TPU v7x, 512 devices: a whole 4x4x16 slice. The times are simulated.
512 devices in a mesh: dp: 8 (over x_hi, y), seq: 64 (over z, x_lo, core).
Axes of the slice: x: 4 (x_hi: 2, x_lo: 2; x = x_hi * 2 + x_lo), y: 4, z: 16, core: 2. Of those that a mesh axis runs over, the one named last changes fastest.
Arguments:
- video: bfloat16 [8, 64, 256, 768], P('dp', 'seq'), may hold values from -6 to 6
- upstream: bfloat16 [8, 64, 256, 768], P('dp', 'seq'), may hold values from -6 to 6
- standardize_scale: float32 [768], replicated, may hold values from 0.25 to 1.75
- ln_bias: float32 [768], replicated, may hold values from -3 to 3
- w_qkv: bfloat16 [768, 2304], P('seq'), may hold values from -0.21875 to 0.21875
- w_out: bfloat16 [768, 768], P('seq'), may hold values from -0.21875 to 0.21875
- windows: float32 [64, 768], replicated, may hold values from -6 to 6
- positives: int32 [64], replicated, may hold values from 0 to 63, each once
Outputs:
- grad_video: bfloat16 [8, 64, 256, 768], P('dp', 'seq')
- grad_out_weight: float32 [512, 1152], P(('dp', 'seq'))
- pooled: float32 [64, 768], replicated
- contrast_loss: float32 [], replicated
Inputs may be any that keep to these rules, and one draw needn't show every extreme that they name: `positives`: each window index is the positive of exactly one clip.
All inputs are finite; a program needn't handle non-finite values.
Results may differ from a plain program's by a relative error of at most 0.0075.
Values may be sent and summed in bfloat16 or wider, within the bound.
A program may use at most 64 MiB of HBM per device.

v0:
```python
import jax
import jax.numpy as jnp
from jax import lax
from jax.sharding import PartitionSpec as P

HEADS = 12
CLIP = 8


sharpness_factor = 1.0 / 0.07


def contrast(pooled_features, windows, positives):
    segment_direction_normalized = (
        pooled_features
        * lax.rsqrt(jnp.mean(pooled_features * pooled_features, -1, keepdims=True) + 1e-06)
        * pooled_features.shape[-1] ** (-0.5)
    )
    span_direction_normalized = (
        windows
        * lax.rsqrt(jnp.mean(windows * windows, -1, keepdims=True) + 1e-06)
        * windows.shape[-1] ** (-0.5)
    )
    cosine_score_matrix = (
        jnp.dot(
            segment_direction_normalized,
            span_direction_normalized.T,
            precision=lax.Precision.HIGHEST,
        )
        * sharpness_factor
    )
    row_lse = jax.nn.logsumexp(cosine_score_matrix, axis=1)
    column_lse = jax.nn.logsumexp(cosine_score_matrix, axis=0)
    matched = positives[:, None] == lax.iota(jnp.int32, cosine_score_matrix.shape[1])[None, :]
    positive = jnp.sum(
        jnp.where(matched, cosine_score_matrix, jnp.zeros_like(cosine_score_matrix)), 1
    )
    return 0.5 * (jnp.mean(row_lse) + jnp.mean(column_lse)) - jnp.mean(positive)


def to_patches(frame_rows):
    return lax.all_to_all(frame_rows, "seq", split_axis=1, concat_axis=0, tiled=True)


def to_frames(patch_rows):
    return lax.all_to_all(patch_rows, "seq", split_axis=0, concat_axis=1, tiled=True)


def layer_norm(tokens, standardize_scale, ln_bias):
    tokens_f = tokens.astype(jnp.float32)
    centered = tokens_f - jnp.mean(tokens_f, -1, keepdims=True)
    inverse_deviation = lax.rsqrt(jnp.mean(centered * centered, -1, keepdims=True) + 1e-06)
    unit = centered * inverse_deviation
    return (
        tokens_f,
        unit,
        inverse_deviation,
        (unit * standardize_scale + ln_bias).astype(jnp.bfloat16),
    )


def attend(query_part, key_part, value_part, scale):
    scores = (
        jnp.einsum("tphd,uphd->phtu", query_part, key_part, preferred_element_type=jnp.float32)
        * scale
    )
    attention_probabilities = jax.nn.softmax(scores, -1)
    probability_half = attention_probabilities.astype(jnp.bfloat16)
    attended_context = jnp.einsum(
        "phtu,uphd->tphd", probability_half, value_part, preferred_element_type=jnp.float32
    ).astype(jnp.bfloat16)
    return (attention_probabilities, probability_half, attended_context)


def attend_back(
    query_part,
    key_part,
    value_part,
    attention_probabilities,
    probability_half,
    derivative_mixed_frames,
    scale,
):
    grad_prob = jnp.einsum(
        "tphd,uphd->phtu", derivative_mixed_frames, value_part, preferred_element_type=jnp.float32
    )
    grad_value = jnp.einsum(
        "phtu,tphd->uphd",
        probability_half,
        derivative_mixed_frames,
        preferred_element_type=jnp.float32,
    ).astype(jnp.bfloat16)
    row_dot = jnp.sum(attention_probabilities * grad_prob, -1, keepdims=True)
    grad_score = (attention_probabilities * (grad_prob - row_dot) * scale).astype(jnp.bfloat16)
    grad_query = jnp.einsum(
        "phtu,uphd->tphd", grad_score, key_part, preferred_element_type=jnp.float32
    ).astype(jnp.bfloat16)
    grad_key = jnp.einsum(
        "phtu,tphd->uphd", grad_score, query_part, preferred_element_type=jnp.float32
    ).astype(jnp.bfloat16)
    return (grad_query, grad_key, grad_value)


def per_device(video, upstream, standardize_scale, ln_bias, w_qkv, w_out, windows, positives):
    frames_dev, patches, width = (video.shape[1], video.shape[2], video.shape[3])
    head_dim = width // HEADS
    scale = head_dim ** (-0.5)
    full_qkv, full_out = (
        lax.all_gather(w_qkv, "seq", axis=0, tiled=True),
        lax.all_gather(w_out, "seq", axis=0, tiled=True),
    )
    tokens_f, unit, inverse_deviation, normed = layer_norm(video[0], standardize_scale, ln_bias)
    qkv = jnp.dot(normed.reshape(-1, width), full_qkv, preferred_element_type=jnp.float32).astype(
        jnp.bfloat16
    )
    qkv = to_patches(qkv.reshape(frames_dev, patches, 3 * width))
    total_frames, local_patches = (qkv.shape[0], qkv.shape[1])
    qkv_parts = qkv.reshape(total_frames, local_patches, 3, HEADS, head_dim)
    query_part, key_part, value_part = (qkv_parts[:, :, 0], qkv_parts[:, :, 1], qkv_parts[:, :, 2])
    attention_probabilities, probability_half, attended_context = attend(
        query_part, key_part, value_part, scale
    )
    context_frames = to_frames(attended_context.reshape(total_frames, local_patches, width))
    context_rows = context_frames.reshape(-1, width)
    output = tokens_f + jnp.dot(context_rows, full_out, preferred_element_type=jnp.float32).reshape(
        frames_dev, patches, width
    )
    clip_count = windows.shape[0]
    clip_slab = frames_dev * lax.axis_size("seq") // CLIP
    clip_index = lax.axis_index("dp") * clip_slab + lax.axis_index("seq") * frames_dev // CLIP
    selector = (lax.iota(jnp.int32, clip_count) == clip_index).astype(jnp.float32)
    partial_sums = selector[:, None] * jnp.sum(output, (0, 1))[None, :]
    pooled_features = lax.psum(partial_sums, ("dp", "seq")) / (CLIP * patches)
    contrast_loss, derivative_averaged_embedding = jax.value_and_grad(contrast)(
        pooled_features, windows, positives
    )
    grad_clip = jnp.sum(selector[:, None] * derivative_averaged_embedding, 0)
    grad_output = upstream[0].astype(jnp.float32) + clip_count * grad_clip[None, None, :]
    grad_rows = grad_output.astype(jnp.bfloat16).reshape(-1, width)
    weight_term = jnp.einsum(
        "rd,re->de", context_rows, grad_rows, preferred_element_type=jnp.float32
    )
    device_count = lax.axis_size(("dp", "seq"))
    grad_out_weight = lax.psum_scatter(
        weight_term.reshape(device_count, -1), ("dp", "seq"), scatter_dimension=0, tiled=True
    )
    derivative_mixed_frames = jnp.einsum(
        "re,de->rd", grad_rows, full_out, preferred_element_type=jnp.float32
    ).astype(jnp.bfloat16)
    derivative_mixed_frames = to_patches(
        derivative_mixed_frames.reshape(frames_dev, patches, width)
    )
    derivative_mixed_frames = derivative_mixed_frames.reshape(
        total_frames, local_patches, HEADS, head_dim
    )
    grad_query, grad_key, grad_value = attend_back(
        query_part,
        key_part,
        value_part,
        attention_probabilities,
        probability_half,
        derivative_mixed_frames,
        scale,
    )
    grad_qkv = jnp.stack([grad_query, grad_key, grad_value], 2).reshape(
        total_frames, local_patches, 3 * width
    )
    grad_qkv_frames = to_frames(grad_qkv)
    grad_normed = jnp.einsum(
        "rc,dc->rd",
        grad_qkv_frames.reshape(-1, 3 * width),
        full_qkv,
        preferred_element_type=jnp.float32,
    ).astype(jnp.bfloat16)
    grad_normed = grad_normed.reshape(frames_dev, patches, width)
    scaled = grad_normed.astype(jnp.float32) * standardize_scale
    grad_norm = inverse_deviation * (
        scaled
        - jnp.mean(scaled, -1, keepdims=True)
        - unit * jnp.mean(scaled * unit, -1, keepdims=True)
    )
    grad_video = (grad_output + grad_norm).astype(jnp.bfloat16)[None]
    return (grad_video, grad_out_weight, pooled_features, contrast_loss)


def solution(mesh):
    in_specs = (
        P("dp", "seq", None, None),
        P("dp", "seq", None, None),
        P(),
        P(),
        P("seq", None),
        P("seq", None),
        P(),
        P(),
    )
    out_specs = (P("dp", "seq", None, None), P(("dp", "seq"), None), P(), P())
    return jax.shard_map(
        per_device, mesh=mesh, in_specs=in_specs, out_specs=out_specs, check_vma=False
    )
```

profile of v0, /device:TPU:1, one launch (start us, length us, event | category | flops | bytes accessed | tf_op | source)
XLA Modules:
  0.0 1352.7 jit_solution(8163083323239953589)
XLA Ops:
  7.2 0.7 all-gather.5.cloned.1.call-update
  7.9 1.1 convert_reduce_fusion
  9.0 1.2 fusion.48
  10.3 131.0 %all-gather.5.cloned.1.call-done = bf16[64,12,2304]{2,1,0:T(8,128)(2,1)} async-done(((bf16[1,12,2304]{2,1,0:T(8,128)(2,1)}), bf16[64,12,2304]{2,1,0:T(8,128)(2,1)}) %all-gather.5.cloned.1.call-update) | async-done | bytes 3538960 | tf_op jit(solution)/shard_map/all_gather | solution.py:109
  141.3 4.9 reshape.282
  146.2 1.7 copy-done
  147.9 2.2 fusion.2
  150.1 1.8 copy.102
  152.4 7.8 reduce.14
  160.3 1.6 reshape.288
  161.9 9.2 all-to-all-start
  171.1 0.7 all-gather.7.cloned.1.call-update
  171.8 60.6 %all-to-all-done = bf16[64,2,4608]{2,1,0:T(2,128)(2,1)S(1)} async-done(((bf16[64,2,4608]{2,1,0:T(2,128)(2,1)}), bf16[64,2,4608]{2,1,0:T(2,128)(2,1)S(1)}, u32[]{:S(2)}, u32[]{:S(2)}) %all-to-all-start) | async-done | bytes 1179680 | tf_op jit(solution)/shard_map/all_to_all | solution.py:42
  232.4 1.0 reshape.289
  233.4 7.8 bitcast_reduce_fusion
  241.2 3.4 reshape.271
  244.6 2.2 fusion.111
  246.8 2.1 copy.79
  248.9 3.9 fusion.112
  252.8 1.8 convolution_convert_fusion.2
  254.5 1.1 copy.58
  255.6 7.2 all-to-all-start.1
  263.0 46.6 %all-gather.7.cloned.1.call-done = bf16[64,12,768]{2,1,0:T(8,128)(2,1)} async-done(((bf16[1,12,768]{2,1,0:T(8,128)(2,1)}), bf16[64,12,768]{2,1,0:T(8,128)(2,1)}) %all-gather.7.cloned.1.call-update) | async-done | bytes 1179664 | tf_op jit(solution)/shard_map/all_gather | solution.py:110
  309.6 2.2 reshape.284
  312.5 0.8 broadcast_multiply_fusion.1
  313.3 453.3 %all-reduce.4.cloned.1.call-done = f32[64,768]{1,0:T(8,128)} async-done(((f32[64,768]{1,0:T(8,128)}), f32[64,768]{1,0:T(8,128)}) %all-reduce.4.cloned.1.call-update) | async-done | bytes 196624 | tf_op jit(solution)/shard_map/psum | solution.py:133
  766.6 1.1 multiply_reduce_fusion.3
  767.7 1.5 fusion.110
  769.3 0.7 select_reduce_fusion
  770.6 0.7 add_reduce_fusion
  773.1 3.0 reduce.15
  776.4 36.6 %all_to_all.16 = bf16[64,2,1536]{2,1,0:T(2,128)(2,1)S(1)} all-to-all(bf16[64,2,1536]{2,1,0:T(2,128)(2,1)S(1)} %reshape.290), channel_id=1, replica_groups=mesh['dp'=8,'seq'=64] {'seq'}, dimensions={0} | all-to-all | bytes 786432 | tf_op jit(solution)/shard_map/all_to_all | solution.py:42
  813.3 2.3 bitcast_reduce_fusion.1
  816.2 1.0 copy.66
  817.2 1.6 fusion.49
  818.8 4.4 fusion.24
  823.2 4.2 fusion.21
  827.4 1.9 fusion.20
  829.4 2.0 pad_maximum_fusion
  831.4 4.1 copy.77
  835.5 2.7 reshape.285
  838.2 4.7 all-to-all-start.3
  843.0 1.6 fusion.56
  844.6 1.7 reshape.278
  848.4 490.3 %all-reduce.6.cloned.1.call-done = f32[512,1152]{1,0:T(8,128)} async-done(((f32[512,1152]{1,0:T(8,128)}), f32[512,1152]{1,0:T(8,128)}) %all-reduce.6.cloned.1.call-update) | async-done | bytes 2359312
  1338.7 1.4 constant_dynamic-slice_fusion
  1340.4 3.3 fusion.109
  1343.8 1.1 fusion.58
  (58 shorter events, 5.4 us)
Async XLA Ops:
  7.2 134.1 %all-gather.5.cloned.1.call-start = ((), (), s32[]{:S(2)}) async-start(), calls=%async_computation.5 | async-start | bytes 4792320 | tf_op jit(solution)/shard_map/all_gather | solution.py:109
  10.3 137.6 %copy-start.12 = (f32[768]{0:T(1024)S(1)}, f32[768]{0:T(1024)}, u32[]{:S(2)}) copy-start(f32[768]{0:T(1024)} %param.11) | copy-start | bytes 9220
  10.3 137.6 %copy-start.13 = (f32[768]{0:T(1024)S(1)}, f32[768]{0:T(1024)}, u32[]{:S(2)}) copy-start(f32[768]{0:T(1024)} %param.10) | copy-start | bytes 9220
  146.2 1.8 copy-start
  161.9 70.5 %all-to-all-start = ((bf16[64,2,4608]{2,1,0:T(2,128)(2,1)}), bf16[64,2,4608]{2,1,0:T(2,128)(2,1)S(1)}, u32[]{:S(2)}, u32[]{:S(2)}) async-start(bf16[64,2,4608]{2,1,0:T(2,128)(2,1)} %reshape.288), calls=%async_computation | async-start | bytes 2359296 | tf_op jit(solution)/shard_map/all_to_all | solution.py:42
  171.1 138.5 %all-gather.7.cloned.1.call-start = ((), (), s32[]{:S(2)}) async-start(), calls=%async_computation.6 | async-start | bytes 1597440 | tf_op jit(solution)/shard_map/all_gather | solution.py:110
  246.8 2.1 copy-start.8
  254.5 8.3 copy-start.4
  255.6 56.2 %all-to-all-start.1 = ((bf16[64,4,768]{2,1,0:T(4,128)(2,1)}), bf16[64,4,768]{2,1,0:T(4,128)(2,1)S(1)}, u32[]{:S(2)}, u32[]{:S(2)}) async-start(bf16[64,4,768]{2,1,0:T(4,128)(2,1)} %copy.58), calls=%async_computation.1 | async-start | bytes 786432 | tf_op jit(solution)/shard_map/all_to_all | solution.py:46
  262.8 503.8 %all-reduce.4.cloned.1.call-start = ((), (), s32[]{:S(2)}) async-start(), calls=%async_computation.4 | async-start | bytes 393216 | tf_op jit(solution)/shard_map/psum | solution.py:133
  263.0 48.9 %copy-start.1 = (bf16[1,1,256,768]{3,2,1,0:T(8,128)(2,1)S(1)}, bf16[1,1,256,768]{3,2,1,0:T(8,128)(2,1)}, u32[]{:S(2)}) copy-start(bf16[1,1,256,768]{3,2,1,0:T(8,128)(2,1)} %param.8) | copy-start | bytes 1179652
  312.0 457.3 %copy-start.5 = (bf16[256,768]{1,0:T(8,128)(2,1)}, bf16[256,768]{1,0:T(8,128)(2,1)S(1)}, u32[]{:S(2)}) copy-start(bf16[256,768]{1,0:T(8,128)(2,1)S(1)} %reshape.273) | copy-start | bytes 1179652
  312.0 457.3 %copy-start.11 = (s32[64]{0:T(128)S(1)}, s32[64]{0:T(128)}, u32[]{:S(2)}) copy-start(s32[64]{0:T(128)} %param.15) | copy-start | bytes 772
  312.5 459.5 %copy-start.6 = (bf16[1,1,256,768]{3,2,1,0:T(8,128)(2,1)S(1)}, bf16[1,1,256,768]{3,2,1,0:T(8,128)(2,1)}, u32[]{:S(2)}) copy-start(bf16[1,1,256,768]{3,2,1,0:T(8,128)(2,1)} %param.9) | copy-start | bytes 1179652
  766.6 5.2 copy-start.3
  767.7 4.8 copy-start.10
  818.8 4.4 copy-start.9
  838.2 501.9 %all-to-all-start.3 = ((bf16[64,4,2304]{2,1,0:T(4,128)(2,1)}), bf16[64,4,2304]{2,1,0:T(4,128)(2,1)S(1)}, u32[]{:S(2)}, u32[]{:S(2)}) async-start(bf16[64,4,2304]{2,1,0:T(4,128)(2,1)} %reshape.285), calls=%async_computation.3 | async-start | bytes 2359296 | tf_op jit(solution)/shard_map/all_to_all | solution.py:46
  843.0 495.8 %all-reduce.6.cloned.1.call-start = ((), (), s32[]{:S(2)}) async-start(), calls=%async_computation.7 | async-start | bytes 4718592
  846.4 494.0 %copy-start.2 = (bf16[1,1,256,768]{3,2,1,0:T(8,128)(2,1)S(1)}, bf16[1,1,256,768]{3,2,1,0:T(8,128)(2,1)}, u32[]{:S(2)}) copy-start(bf16[1,1,256,768]{3,2,1,0:T(8,128)(2,1)} %param.8) | copy-start | bytes 1179652
  1340.4 3.3 copy-start.7
Sparse Core Ops, SparseCore 0:
  10.1 131.0 all-gather.4
  174.1 135.4 all-gather.6
  315.6 450.9 all-reduce.3
  849.6 489.0 all-reduce.5
where the time goes:
time: 1360 us; the launch traced here: 1350 us
  waiting for transfers between devices  1180 us (87%)
  local copies, waits for them, and re-layouts  45.7 us (3%)
  blocking collectives  36.6 us (3%)
  matrix products  27.8 us (2%)
  starting transfers between devices  21.3 us (2%)
  other arithmetic  20.5 us (2%)
  between operations  17.6 us (1%)
    unnamed x5, waiting for transfers between devices  492 us
    psum x1, waiting for transfers between devices, per_device(): pooled_features = lax.psum(partial_sums, ('dp', 'seq')) / (CLIP * patches)  453 us
    all_gather x1, waiting for transfers between devices, per_device(): lax.all_gather(w_qkv, 'seq', axis=0, tiled=True)  131 us
    all_to_all x1, waiting for transfers between devices, to_patches(): lax.all_to_all(frame_rows, 'seq', split_axis=1, concat_axis=0, tiled=True)  60.6 us
    all_gather x1, waiting for transfers between devices, per_device(): lax.all_gather(w_out, 'seq', axis=0, tiled=True)  46.6 us
    all_to_all x1, blocking collectives, to_patches(): lax.all_to_all(frame_rows, 'seq', split_axis=1, concat_axis=0, tiled=True)  36.6 us
  transfers between devices with their start and end apart: 7, of which 5 were waited for; matrix products, arithmetic and copies ran while one was open for 2% of the time, Pallas kernels for 0%

commit v1 on v0

v1 whole, which is shorter than its diff:
```python
import jax
import jax.numpy as jnp
from jax import lax
from jax.experimental import pallas as pl
from jax.experimental.pallas import tpu as pltpu
from jax.sharding import PartitionSpec as P

MESH = pl.DeviceIdType.MESH
F32 = jnp.float32
BF16 = jnp.bfloat16
D = 768
EPS = 1e-6
NEG = -1e30
SHARP = 1.0 / 0.07
VMEM_LIMIT = 56 * 1024 * 1024


class Place:
    def __init__(self):
        self.dp = lax.axis_index("dp")
        self.seq = lax.axis_index("seq")
        self.x_hi = self.dp // 4
        self.y = self.dp % 4
        self.z = self.seq // 4
        self.role = self.seq % 4
        self.x_lo = self.role // 2
        self.core = self.seq % 2
        self.k = self.seq // 2
        self.x = self.x_hi * 2 + self.x_lo
        self.m = self.dp * 4 + self.role


def send(src, dst, send_sem, recv_sem, dp, seq):
    pltpu.make_async_remote_copy(
        src_ref=src,
        dst_ref=dst,
        send_sem=send_sem,
        recv_sem=recv_sem,
        device_id=(dp, seq),
        device_id_type=MESH,
    ).start()


def drain(ref, sem):
    pltpu.make_async_copy(ref, ref, sem).wait()


def barrier(me):
    sem = pltpu.get_barrier_semaphore()

    def slab(i, carry):
        to = lax.rem(me.k + i, 32) * 2 + me.core
        pl.semaphore_signal(sem, inc=1, device_id=(me.dp, to), device_id_type=MESH)
        return carry

    def plane(i, carry):
        to = lax.rem(me.m + i, 32)
        pl.semaphore_signal(
            sem, inc=1, device_id=(to // 4, me.z * 4 + to % 4), device_id_type=MESH
        )
        return carry

    lax.fori_loop(1, 32, slab, 0)
    lax.fori_loop(1, 32, plane, 0)
    pl.semaphore_wait(sem, 62)


def dot(a, b):
    return lax.dot_general(a, b, (((1,), (0,)), ((), ())), preferred_element_type=F32)


def dot_nt(a, b):
    return lax.dot_general(a, b, (((1,), (1,)), ((), ())), preferred_element_type=F32)


def dot_tn(a, b):
    return lax.dot_general(a, b, (((0,), (0,)), ((), ())), preferred_element_type=F32)


def iota(shape, dim):
    return lax.broadcasted_iota(jnp.int32, shape, dim)


def one_hot(condition):
    return jnp.where(condition, 1.0, 0.0).astype(BF16)


def gather_order():
    j = iota((1, D), 1)
    block, rest = j // 96, j % 96
    core, half, x_lo = block // 4, (block // 2) % 2, block % 2
    z8, r = rest // 12, rest % 12
    natural = ((half * 8 + z8) * 4 + x_lo * 2 + core) * 12 + r
    return one_hot(iota((D, D), 0) == natural)


def scatter_order():
    j = iota((1, D), 1)
    dp, rest = j // 96, j % 96
    x_lo, z, r = rest // 48, (rest % 48) // 3, rest % 3
    natural = dp * 96 + z * 6 + x_lo * 3 + r
    return one_hot(iota((D, D), 0) == natural)


def split3(a):
    high = a.astype(BF16)
    rest = a - high.astype(F32)
    mid = rest.astype(BF16)
    low = (rest - mid.astype(F32)).astype(BF16)
    return jnp.concatenate([high.astype(F32), mid.astype(F32), low.astype(F32)], 0).astype(BF16)


def start_tokens(me, src, buf, local_sem, send_sem, recv_sem):
    pltpu.make_async_copy(src.at[me.k], buf.at[me.k], local_sem).start()

    def step(i, carry):
        offset = jnp.where(i % 2 == 0, 32 - i // 2, (i + 1) // 2)
        to = lax.rem(me.k + offset, 32)
        send(src.at[to], buf.at[me.k], send_sem, recv_sem, me.dp, to * 2 + me.core)
        return carry

    lax.fori_loop(1, 32, step, 0)


def wait_tokens(me, src, buf, local_sem, recv_sem):
    pltpu.make_async_copy(src.at[me.k], buf.at[me.k], local_sem).wait()
    drain(buf.at[pl.ds(0, 31)], recv_sem)


def start_pair(me, buf, out, box, send_sem, recv_sem):
    rows = buf[...].astype(F32).reshape(256, D).astype(BF16)
    r, col = iota((128, 1), 0), iota((128, 256), 1)
    at = (r % 32) * 8 + r // 32
    theirs = dot(one_hot(col == at + 4 * (1 - me.core)), rows)
    box[...] = theirs.astype(BF16).reshape(4, 32, D)
    send(box, out.at[me.core], send_sem, recv_sem, me.dp, me.seq + 1 - 2 * me.core)
    mine = dot(one_hot(col == at + 4 * me.core), rows)
    out[me.core] = mine.astype(BF16).reshape(4, 32, D)


def start_weights_z(me, piece, buf, local_sem, send_sem, recv_sem):
    pltpu.make_async_copy(piece, buf.at[me.z], local_sem).start()

    def step(i, carry):
        to = lax.rem(me.z + i, 16)
        send(piece, buf.at[me.z], send_sem, recv_sem, me.dp, to * 4 + me.role)
        return carry

    lax.fori_loop(1, 16, step, 0)


def start_weights_first(me, piece, buf, full, local_sem, recv_z, send_sem, recv_a, recv_b):
    pltpu.make_async_copy(piece, buf.at[me.z], local_sem).wait()
    drain(buf.at[pl.ds(0, 15)], recv_z)
    rows = buf[...].reshape(256, 384)
    r = iota((192, 1), 0)
    pick = one_hot(iota((192, 256), 1) == (r // 12) * 16 + r % 12)
    block = dot(pick, rows).astype(BF16)
    full[me.x_hi, me.y, me.core, 0, me.x_lo] = block[:96]
    full[me.x_hi, me.y, me.core, 1, me.x_lo] = block[96:]
    mine = full.at[me.x_hi, me.y, me.core, 0, me.x_lo]
    for i in range(1, 4):
        x = lax.rem(me.x + i, 4)
        send(mine, mine, send_sem, recv_a, (x // 2) * 4 + me.y, me.z * 4 + (x % 2) * 2 + me.core)
    mine = full.at[me.x_hi, me.y, me.core, 1, me.x_lo]
    for i in range(1, 4):
        y = lax.rem(me.y + i, 4)
        send(mine, mine, send_sem, recv_b, me.x_hi * 4 + y, me.seq)


def start_weights_second(me, full, recv_a, recv_b, send_sem, recv_a2, recv_b2, send_pair, recv_pair):
    pair = me.seq + 1 - 2 * me.core
    drain(full.at[0, pl.ds(0, 3), 0, 0, 0], recv_a)
    mine = full.at[:, me.y, me.core, 0]
    for i in range(1, 4):
        y = lax.rem(me.y + i, 4)
        send(mine, mine, send_sem, recv_a2.at[i - 1], me.x_hi * 4 + y, me.seq)
    send(mine, mine, send_pair, recv_pair, me.dp, pair)
    drain(full.at[0, pl.ds(0, 3), 0, 0, 0], recv_b)
    mine = full.at[me.x_hi, :, me.core, 1, me.x_lo]
    for i in range(1, 4):
        x = lax.rem(me.x + i, 4)
        send(
            mine, mine, send_sem, recv_b2.at[i - 1],
            (x // 2) * 4 + me.y, me.z * 4 + (x % 2) * 2 + me.core,
        )
    send(mine, mine, send_pair, recv_pair, me.dp, pair)


def finish_weights(me, full, recv_a2, recv_b2, send_pair, recv_pair):
    pair = me.seq + 1 - 2 * me.core
    for i in range(1, 4):
        y = lax.rem(me.y + 4 - i, 4)
        block = full.at[:, y, me.core, 0]
        drain(block, recv_a2.at[i - 1])
        send(block, block, send_pair, recv_pair, me.dp, pair)
        x = lax.rem(me.x + 4 - i, 4)
        block = full.at[x // 2, :, me.core, 1, x % 2]
        drain(block, recv_b2.at[i - 1])
        send(block, block, send_pair, recv_pair, me.dp, pair)
    drain(full.at[:, :, 0], recv_pair)


def reduce_pooled(me, part, box1, in1, buf2, pool, send_sem, recv1, recv2, recv3):
    for q in range(4):
        box1[q] = part[2 * q : 2 * q + 2, :]
    in1[me.role] = box1[me.role]
    for i in range(1, 4):
        to = lax.rem(me.role + i, 4)
        send(box1.at[to], in1.at[me.role], send_sem.at[0], recv1, me.dp, me.z * 4 + to)
    drain(in1.at[pl.ds(0, 3)], recv1)
    buf2[me.z] = jnp.sum(in1[...], 0)

    def along_z(i, carry):
        to = lax.rem(me.z + i, 16)
        send(buf2.at[me.z], buf2.at[me.z], send_sem.at[1], recv2, me.dp, to * 4 + me.role)
        return carry

    lax.fori_loop(1, 16, along_z, 0)
    drain(buf2.at[pl.ds(0, 15)], recv2)
    pool[me.m] = jnp.sum(buf2[...], 0) * (1.0 / 2048.0)

    def in_plane(i, carry):
        to = lax.rem(me.m + i, 32)
        send(pool.at[me.m], pool.at[me.m], send_sem.at[2], recv3, to // 4, me.z * 4 + to % 4)
        return carry

    lax.fori_loop(1, 32, in_plane, 0)
    drain(pool.at[pl.ds(0, 31)], recv3)
    drain(in1.at[pl.ds(0, 3)], send_sem.at[0])
    drain(buf2.at[pl.ds(0, 15)], send_sem.at[1])
    drain(pool.at[pl.ds(0, 31)], send_sem.at[2])


def start_weight_sum(me, box, buf, send_sem, recv_sem):
    buf[me.m] = box[me.m]

    def step(i, carry):
        to = lax.rem(me.m + i, 32)
        send(box.at[to], buf.at[me.m], send_sem, recv_sem, to // 4, me.z * 4 + to % 4)
        return carry

    lax.fori_loop(1, 32, step, 0)


def second_weight_sum(me, buf, recv_sem, box_z, buf_z, send_sem, recv_z):
    drain(buf.at[pl.ds(0, 31)], recv_sem)
    total = lax.fori_loop(
        0, 32, lambda i, t: t + buf[i].astype(F32), jnp.zeros((48, 384), F32)
    )
    box_z[...] = jnp.zeros_like(box_z)
    for z in range(16):
        box_z[z, 0:3, :] = total[3 * z : 3 * z + 3, :]
    buf_z[me.z] = box_z[me.z]

    def step(i, carry):
        to = lax.rem(me.z + i, 16)
        send(box_z.at[to], buf_z.at[me.z], send_sem, recv_z, me.dp, to * 4 + me.role)
        return carry

    lax.fori_loop(1, 16, step, 0)


def third_weight_sum(me, buf_z, recv_z, rows, send_sem, recv_sem):
    drain(buf_z.at[pl.ds(0, 15)], recv_z)
    rows[me.core] = jnp.sum(buf_z[...], 0)
    send(
        rows.at[me.core], rows.at[me.core], send_sem, recv_sem,
        me.dp, me.seq + 1 - 2 * me.core,
    )


def finish_weight_sum(me, rows, recv_sem, out):
    drain(rows.at[0], recv_sem)
    left, right = rows[0], rows[1]
    first = me.core == 0
    out[0:1, 0:384] = jnp.where(first, left[0:1], right[1:2])
    out[0:1, 384:768] = jnp.where(first, right[0:1], left[2:3])
    out[0:1, 768:1152] = jnp.where(first, left[1:2], right[2:3])


def start_back_pair(me, grads, buf, send_sem, recv_sem):
    theirs = 1 - me.core
    send(grads.at[theirs], buf.at[me.core], send_sem, recv_sem, me.dp, me.seq + 1 - 2 * me.core)
    buf[me.core] = grads[me.core]


def start_back(me, buf, recv_pair, box, out, local_sem, send_sem, recv_sem):
    drain(buf.at[0], recv_pair)
    r = iota((256, 1), 0)
    at = ((r // 4) % 2) * 128 + (r % 4) * 32 + r // 8
    rows = dot(one_hot(iota((256, 256), 1) == at), buf[...].reshape(256, D))
    box[...] = rows.reshape(32, 8, D).astype(BF16)
    start_tokens(me, box, out, local_sem, send_sem, recv_sem)


def normalize(x):
    centered = x - jnp.mean(x, -1, keepdims=True)
    inverse = lax.rsqrt(jnp.mean(centered * centered, -1, keepdims=True) + EPS)
    return centered * inverse, inverse


def clip_pick():
    return one_hot((iota((8, 256), 1) % 32) // 4 == iota((8, 256), 0))


def unit_rows(ref, u, columns):
    return jnp.concatenate(
        [ref[u * 64 : u * 64 + 64, columns], ref[128 + u * 64 : 192 + u * 64, columns]], 0
    )


def put_rows(ref, u, columns, value):
    ref[u * 64 : u * 64 + 64, columns] = value[:64]
    ref[128 + u * 64 : 192 + u * 64, columns] = value[64:]


def heads(a):
    even = iota(a.shape, 1) < 64
    zero = jnp.zeros_like(a)
    return jnp.concatenate([jnp.where(even, a, zero), jnp.where(even, zero, a)], 0)


def same_patch():
    return (iota((256, 128), 0) // 32) % 2 == (iota((256, 128), 1) // 32) % 2


def forward(tokens, full, scale, bias, order, qkv, prob, context, part):
    x = tokens[...].reshape(256, D)
    unit, _ = normalize(x.astype(F32))
    normed = (unit * scale[...] + bias[...]).astype(BF16)
    normed = dot(normed, order[...]).astype(BF16)
    for n in range(6):
        weight = full[n // 4, n % 4].reshape(D, 384)
        qkv[:, n * 384 : n * 384 + 384] = dot(normed, weight).astype(BF16)
    keep = same_patch()
    for j in range(6):
        for u in range(2):
            columns = [slice(s * D + j * 128, s * D + j * 128 + 128) for s in range(3)]
            query, key, value = [unit_rows(qkv, u, c) for c in columns]
            score = dot_nt(heads(query), key) * 0.125
            score = jnp.where(keep, score, NEG)
            top = jnp.max(score, -1, keepdims=True)
            weight = jnp.exp(score - top)
            p = weight / jnp.sum(weight, -1, keepdims=True)
            prob[j * 2 + u] = p
            half = p.astype(BF16)
            both = jnp.concatenate([half[:128], half[128:]], 1)
            mixed = dot(both, heads(value)).astype(BF16)
            put_rows(context, u, slice(j * 128, j * 128 + 128), mixed)
    pick = clip_pick()
    ctx_sum = split3(dot(pick, context[...]))
    ctx_sum = dot(ctx_sum, order[...]).astype(BF16)
    sums = dot(pick, x)
    for n in range(2):
        weight = full[1, 2 + n].reshape(D, 384)
        s = dot(ctx_sum, weight)
        columns = slice(n * 384, n * 384 + 384)
        part[:, columns] = sums[:, columns] + s[0:8] + s[8:16] + s[16:24]


def spread(upstream, grad_clip):
    pick = one_hot((iota((256, 24), 0) % 32) // 4 == iota((256, 24), 1) % 8)
    return upstream[...].reshape(256, D).astype(F32) + dot(pick, split3(grad_clip))


def backward_weights(grad_half, full, order, scatter, context, grad_context, box):
    back = dot_nt(grad_half[:, :384], full[1, 2].reshape(D, 384))
    back = back + dot_nt(grad_half[:, 384:], full[1, 3].reshape(D, 384))
    grad_context[...] = dot_nt(back.astype(BF16), order[...]).astype(BF16)
    ordered = dot(context[...], scatter[...]).astype(BF16)
    term = dot_tn(ordered, grad_half).astype(BF16)
    for n in range(16):
        for c in range(2):
            box[n * 2 + c] = term[n * 48 : n * 48 + 48, c * 384 : c * 384 + 384]


def backward_attention(qkv, prob, grad_context, grad_qkv):
    for j in range(6):
        for u in range(2):
            columns = [slice(s * D + j * 128, s * D + j * 128 + 128) for s in range(3)]
            query, key, value = [unit_rows(qkv, u, c) for c in columns]
            grad = heads(unit_rows(grad_context, u, slice(j * 128, j * 128 + 128)))
            p = prob[j * 2 + u]
            half = p.astype(BF16)
            grad_prob = dot_nt(grad, value)
            grad_value = dot_tn(half, grad).astype(BF16)
            row = jnp.sum(p * grad_prob, -1, keepdims=True)
            grad_score = (p * (grad_prob - row) * 0.125).astype(BF16)
            both = jnp.concatenate([grad_score[:128], grad_score[128:]], 1)
            put_rows(grad_qkv, u, columns[0], dot(both, heads(key)).astype(BF16))
            put_rows(grad_qkv, u, columns[1], dot_tn(grad_score, heads(query)).astype(BF16))
            put_rows(grad_qkv, u, columns[2], grad_value)


def backward_tokens(tokens, grad_output, grad_qkv, full, order, scale, out):
    back = jnp.zeros((256, D), F32)
    for n in range(6):
        weight = full[n // 4, n % 4].reshape(D, 384)
        back = back + dot_nt(grad_qkv[:, n * 384 : n * 384 + 384], weight)
    grad_normed = dot_nt(back.astype(BF16), order[...])
    scaled = grad_normed * scale[...]
    unit, inverse = normalize(tokens[...].reshape(256, D).astype(F32))
    grad_norm = inverse * (
        scaled
        - jnp.mean(scaled, -1, keepdims=True)
        - unit * jnp.mean(scaled * unit, -1, keepdims=True)
    )
    out[...] = (grad_output + grad_norm).astype(BF16).reshape(2, 4, 32, D)


def kernel_in(
    video, upstream, piece, tokens, ups, full,
    vbuf, ubuf, vbox, ubox, zbuf, local, tok_send, tok_recv, pair_send, pair_recv,
    w_send, w_recv, w_recv_a2, w_recv_b2, wp_send, wp_recv,
):
    me = Place()
    barrier(me)
    start_weights_z(me, piece, zbuf, local.at[0], w_send.at[0], w_recv.at[0])
    start_tokens(me, video, vbuf, local.at[1], tok_send.at[0], tok_recv.at[0])
    start_weights_first(
        me, piece, zbuf, full, local.at[0], w_recv.at[0], w_send.at[1], w_recv.at[1], w_recv.at[2]
    )
    start_tokens(me, upstream, ubuf, local.at[2], tok_send.at[1], tok_recv.at[1])
    start_weights_second(
        me, full, w_recv.at[1], w_recv.at[2], w_send.at[2], w_recv_a2, w_recv_b2, wp_send, wp_recv
    )
    wait_tokens(me, video, vbuf, local.at[1], tok_recv.at[0])
    start_pair(me, vbuf, tokens, vbox, pair_send.at[0], pair_recv.at[0])
    finish_weights(me, full, w_recv_a2, w_recv_b2, wp_send, wp_recv)
    wait_tokens(me, upstream, ubuf, local.at[2], tok_recv.at[1])
    start_pair(me, ubuf, ups, ubox, pair_send.at[1], pair_recv.at[1])
    drain(tokens.at[0], pair_recv.at[0])
    drain(ups.at[0], pair_recv.at[1])
    drain(zbuf.at[pl.ds(0, 15)], w_send.at[0])
    drain(full.at[0, pl.ds(0, 3), 0, 0], w_send.at[1])
    drain(full.at[0, pl.ds(0, 3)], w_send.at[2])
    drain(full.at[:, :, 0], wp_send)
    for i in range(2):
        drain(vbuf.at[pl.ds(0, 31)], tok_send.at[i])
        drain(vbox, pair_send.at[i])


def kernel_forward(tokens, full, scale, bias, order, qkv, prob, context, part):
    forward(tokens, full, scale, bias, order, qkv, prob, context, part)


def kernel_pooled(part, pooled, box1, in1, buf2, pool, send_sem, recv_sem):
    me = Place()
    barrier(me)
    reduce_pooled(
        me, part, box1, in1, buf2, pool, send_sem, recv_sem.at[0], recv_sem.at[1], recv_sem.at[2]
    )
    for m in range(32):
        pooled[2 * m : 2 * m + 2, :] = pool[m]


def kernel_backward(
    tokens, ups, full, scale, order, scatter, qkv, prob, context, grad_clip, grads, box,
    grad_context, grad_qkv, grad_out,
):
    grad_out[...] = spread(ups, grad_clip[...])
    backward_weights(
        grad_out[...].astype(BF16), full, order, scatter, context, grad_context, box
    )
    backward_attention(qkv, prob, grad_context, grad_qkv)
    backward_tokens(tokens, grad_out[...], grad_qkv, full, order, scale, grads)


def kernel_out(
    grads, box, video_out, weight_out,
    pair_buf, out_box, gw_buf, box_z, buf_z, rows, local, send_sem, recv_sem,
):
    me = Place()
    barrier(me)
    start_back_pair(me, grads, pair_buf, send_sem.at[0], recv_sem.at[0])
    start_weight_sum(me, box, gw_buf, send_sem.at[1], recv_sem.at[1])
    start_back(
        me, pair_buf, recv_sem.at[0], out_box, video_out, local, send_sem.at[2], recv_sem.at[2]
    )
    second_weight_sum(me, gw_buf, recv_sem.at[1], box_z, buf_z, send_sem.at[3], recv_sem.at[3])
    third_weight_sum(me, buf_z, recv_sem.at[3], rows, send_sem.at[4], recv_sem.at[4])
    finish_weight_sum(me, rows, recv_sem.at[4], weight_out)
    wait_tokens(me, out_box, video_out, local, recv_sem.at[2])
    drain(pair_buf.at[0], send_sem.at[0])
    drain(gw_buf.at[pl.ds(0, 31)], send_sem.at[1])
    drain(out_box.at[pl.ds(0, 31)], send_sem.at[2])
    drain(box_z.at[pl.ds(0, 15)], send_sem.at[3])
    drain(rows.at[0], send_sem.at[4])


def shape(*dims, dtype=BF16):
    return jax.ShapeDtypeStruct(dims, dtype)


def call(kernel, outs, ins, out_spaces, in_spaces, scratch, collective=None):
    params = dict(vmem_limit_bytes=VMEM_LIMIT)
    if collective is not None:
        params.update(collective_id=collective, has_side_effects=True)
    return pl.pallas_call(
        kernel,
        out_shape=outs,
        in_specs=[pl.BlockSpec(memory_space=s) for s in in_spaces],
        out_specs=[pl.BlockSpec(memory_space=s) for s in out_spaces],
        scratch_shapes=scratch,
        compiler_params=pltpu.CompilerParams(**params),
    )(*ins)


def contrast(pooled, windows, positives):
    root = D ** (-0.5)
    clip_unit = pooled * lax.rsqrt(jnp.mean(pooled * pooled, -1, keepdims=True) + EPS) * root
    window_unit = windows * lax.rsqrt(jnp.mean(windows * windows, -1, keepdims=True) + EPS) * root
    logits = jnp.dot(clip_unit, window_unit.T, precision=lax.Precision.HIGHEST) * SHARP
    matched = positives[:, None] == lax.iota(jnp.int32, logits.shape[1])[None, :]
    positive = jnp.sum(jnp.where(matched, logits, jnp.zeros_like(logits)), 1)
    row_lse = jax.nn.logsumexp(logits, axis=1)
    column_lse = jax.nn.logsumexp(logits, axis=0)
    return 0.5 * (jnp.mean(row_lse) + jnp.mean(column_lse)) - jnp.mean(positive)


def per_device(video, upstream, standardize_scale, ln_bias, w_qkv, w_out, windows, positives):
    V, A = pltpu.VMEM, pl.ANY
    dma = pltpu.SemaphoreType.DMA
    dp = lax.axis_index("dp")
    scale, bias = standardize_scale.reshape(1, D), ln_bias.reshape(1, D)
    both = jnp.concatenate([w_qkv, w_out], 1)
    piece = jnp.pad(lax.dynamic_slice(both, (0, dp * 384), (12, 384)), ((0, 4), (0, 0)))
    order, scatter = gather_order(), scatter_order()
    tokens, ups, full = call(
        kernel_in,
        [shape(2, 4, 32, D), shape(2, 4, 32, D), shape(2, 4, 2, 2, 2, 96, 384)],
        [video.reshape(32, 8, D), upstream.reshape(32, 8, D), piece],
        [V, V, V],
        [A, A, V],
        [
            V((32, 8, D), BF16), V((32, 8, D), BF16), V((4, 32, D), BF16), V((4, 32, D), BF16),
            V((16, 16, 384), BF16), dma((3,)), dma((2,)), dma((2,)), dma((2,)), dma((2,)),
            dma((3,)), dma((3,)), dma((3,)), dma((3,)), dma, dma,
        ],
        collective=1,
    )
    qkv, prob, context, part = call(
        kernel_forward,
        [shape(256, 3 * D), shape(12, 256, 128, dtype=F32), shape(256, D), shape(8, D, dtype=F32)],
        [tokens, full, scale, bias, order],
        [V] * 4,
        [V] * 5,
        [],
    )
    (pooled,) = call(
        kernel_pooled,
        [shape(64, D, dtype=F32)],
        [part],
        [V],
        [V],
        [
            V((4, 2, D), F32), V((4, 2, D), F32), V((16, 2, D), F32), V((32, 2, D), F32),
            dma((3,)), dma((3,)),
        ],
        collective=2,
    )
    contrast_loss, grad_pooled = jax.value_and_grad(contrast)(pooled, windows, positives)
    grad_clip = 64.0 * lax.dynamic_slice(grad_pooled, (dp * 8, 0), (8, D))
    grads, box = call(
        kernel_backward,
        [shape(2, 4, 32, D), shape(32, 48, 384)],
        [tokens, ups, full, scale, order, scatter, qkv, prob, context, grad_clip],
        [V, V],
        [V] * 10,
        [V((256, D), BF16), V((256, 3 * D), BF16), V((256, D), F32)],
    )
    grad_video, grad_out_weight = call(
        kernel_out,
        [shape(32, 8, D), shape(1, 1152, dtype=F32)],
        [grads, box],
        [A, V],
        [V, V],
        [
            V((2, 4, 32, D), BF16), V((32, 8, D), BF16), V((32, 48, 384), BF16),
            V((16, 4, 384), F32), V((16, 4, 384), F32), V((2, 4, 384), F32),
            dma, dma((5,)), dma((5,)),
        ],
        collective=3,
    )
    return grad_video.reshape(1, 1, 256, D), grad_out_weight, pooled, contrast_loss


def solution(mesh):
    in_specs = (
        P("dp", "seq", None, None),
        P("dp", "seq", None, None),
        P(),
        P(),
        P("seq", None),
        P("seq", None),
        P(),
        P(),
    )
    out_specs = (P("dp", "seq", None, None), P(("dp", "seq"), None), P(), P())
    return jax.shard_map(
        per_device, mesh=mesh, in_specs=in_specs, out_specs=out_specs, check_vma=False
    )
```

time: 1360 us -> 175 us (0.13)
  waiting for transfers between devices: 1180 us -> 0 us
  Pallas kernels: 0 us -> 150 us
  local copies, waits for them, and re-layouts: 45.7 us -> 7.05 us
  blocking collectives: 36.6 us -> 0 us
  matrix products: 27.8 us -> 2.86 us
  starting transfers between devices: 21.3 us -> 0 us
  between operations: 17.6 us -> 3.83 us
    unnamed x5 -> x0, waiting for transfers between devices: 492 us -> none
    psum x1 -> x0, waiting for transfers between devices: 453 us -> none  [per_device(): pooled_features = lax.psum(partial_sums, ('dp', 'seq')) / (CLIP * patches)]
    all_gather x2 -> x0, waiting for transfers between devices: 178 us -> none  [the longest x1 131 us: per_device(): lax.all_gather(w_qkv, 'seq', axis=0, tiled=True)]
    pallas_call x0 -> x5, Pallas kernels: none -> 150 us  [call(): pl.pallas_call(kernel, out_shape=outs, in_specs=[pl.BlockSpec(memory_spac...]
    all_to_all x3 -> x0, waiting for transfers between devices: 60.6 us -> none  [the longest x1 60.6 us: to_patches(): lax.all_to_all(frame_rows, 'seq', split_axis=1, concat_axis=0, tiled=True)]
    all_to_all x1 -> x0, blocking collectives: 36.6 us -> none  [to_patches(): lax.all_to_all(frame_rows, 'seq', split_axis=1, concat_axis=0, tiled=True)]
    dot_general x12 -> x2, matrix products: 24 us -> 2.86 us  [contrast(): jnp.dot(clip_unit, window_unit.T, precision=lax.Precision.HIGHEST) * SHARP]
    all_to_all x3 -> x0, starting transfers between devices: 21.1 us -> none  [the longest x2 11.9 us: to_frames(): lax.all_to_all(patch_rows, 'seq', split_axis=0, concat_axis=1, tiled=True)]
  transfers between devices with their start and end apart: 7 -> 0, of which waited for: 5 -> 0; matrix products, arithmetic and copies ran while one was open for 2% -> 0% of each run, Pallas kernels for 0% -> 0%
where the time goes in v1:
time: 175 us; the launch traced here: 173 us
  Pallas kernels  150 us (86%)
  other arithmetic  9.15 us (5%)
  local copies, waits for them, and re-layouts  7.05 us (4%)
  between operations  3.83 us (2%)
  matrix products  2.86 us (2%)
    pallas_call x5, Pallas kernels, call(): pl.pallas_call(kernel, out_shape=outs, in_specs=[pl.BlockSpec(memory_spac...  150 us
    unnamed x9, local copies, waits for them, and re-layouts  3.74 us

profile of v1, /device:TPU:1, one launch (start us, length us, event | category | flops | bytes accessed | tf_op | source)
XLA Modules:
  0.0 172.8 jit_solution(7118235620177921263)
XLA Ops:
  0.6 1.0 multiply_reduce_fusion.1
  1.7 1.3 reshape.292.scale
  3.0 1.3 reshape.293.bias
  4.3 0.7 fusion.25
  5.0 0.6 pad.4.piece
  5.6 1.4 select_convert_fusion.1.order
  7.1 1.5 select_convert_fusion.scatter
  8.6 69.1 %shard_map.111 = (bf16[2,4,32,768]{3,2,1,0:T(8,128)(2,1)}, bf16[2,4,32,768]{3,2,1,0:T(8,128)(2,1)}, bf16[2,4,2,2,2,96,384]{6,5,4,3,2,1,0:T(8,128)(2,1)}) custom-call(bf16[32,8,768]{2,1,0:T(8,128)(2,1)} %bitcast.3, bf16[32,8,768]{2,1,0:T(8,128)(2,1)} %bitcast.4, bf16[16,384]{1,0:T(8,128)(2,1)} %pad.4.piece), custom_call_target="tpu_custom_call" | custom-call | tf_op jit(solution)/shard_map/pallas_call | solution.py:500
  77.7 0.0 copy-start.1
  77.7 0.0 copy-start.2
  77.7 7.1 %shard_map.112 = (bf16[256,2304]{1,0:T(8,128)(2,1)}, f32[12,256,128]{2,1,0:T(8,128)}, bf16[256,768]{1,0:T(8,128)(2,1)}, f32[8,768]{1,0:T(8,128)}) custom-call(bf16[2,4,32,768]{3,2,1,0:T(8,128)(2,1)} %get-tuple-element.15.tokens, bf16[2,4,2,2,2,96,384]{6,5,4,3,2,1,0:T(8,128)(2,1)} %get-tuple-element.17.full, f32[1,768]{1,0:T(1,128)} %reshape.292.scale, ...), custom_call_target="tpu_custom_call" | custom-call | tf_op jit(solution)/shard_map/pallas_call | solution.py:500
  84.9 25.1 %shard_map.113 = f32[64,768]{1,0:T(8,128)} custom-call(f32[8,768]{1,0:T(8,128)} %get-tuple-element.21.part), custom_call_target="tpu_custom_call" | custom-call | tf_op jit(solution)/shard_map/pallas_call | solution.py:500
  109.9 1.0 multiply_reduce_fusion.2
  111.0 0.0 copy-done.1
  111.0 1.4 fusion.79
  112.5 0.0 copy-done.2
  112.5 0.7 select_reduce_fusion
  113.8 0.6 add_reduce_fusion.1
  114.4 0.6 add_reduce_fusion
  116.3 1.4 multiply_reduce_fusion
  117.8 0.1 dynamic-slice
  117.9 0.1 dynamic-slice.1
  117.9 1.4 fusion.16.grad_clip
  119.4 12.1 %shard_map.114 = (bf16[2,4,32,768]{3,2,1,0:T(8,128)(2,1)}, bf16[32,48,384]{2,1,0:T(8,128)(2,1)}) custom-call(bf16[2,4,32,768]{3,2,1,0:T(8,128)(2,1)} %get-tuple-element.15.tokens, bf16[2,4,32,768]{3,2,1,0:T(8,128)(2,1)} %get-tuple-element.16.ups, bf16[2,4,2,2,2,96,384]{6,5,4,3,2,1,0:T(8,128)(2,1)} %get-tuple-element.17.full, f32[1,768]{1,0:T(1,128)} %reshape.292.scale, ...), custom_call_target="tpu_custom_call" | custom-call | tf_op jit(solution)/shard_map/pallas_call | solution.py:500
  131.4 0.0 copy-start
  131.4 36.5 %shard_map.115 = (bf16[32,8,768]{2,1,0:T(8,128)(2,1)}, f32[1,1152]{1,0:T(1,128)}) custom-call(bf16[2,4,32,768]{3,2,1,0:T(8,128)(2,1)} %get-tuple-element.22.grads, bf16[32,48,384]{2,1,0:T(8,128)(2,1)} %get-tuple-element.23.box), custom_call_target="tpu_custom_call" | custom-call | tf_op jit(solution)/shard_map/pallas_call | solution.py:500
  167.9 1.8 %copy.15 = bf16[1,1,256,768]{3,2,1,0:T(8,128)(2,1)} copy(bf16[1,1,256,768]{3,2,1,0:T(8,128)(2,1)} %bitcast.5) | data formatting | bytes 786432
  169.7 1.3 copy.16
  171.0 0.0 copy-done
  171.0 0.7 copy.17
  (6 shorter events, 0.1 us)
Async XLA Ops:
  77.7 33.3 %copy-start.1 = (f32[64,768]{1,0:T(8,128)S(1)}, f32[64,768]{1,0:T(8,128)}, u32[]{:S(2)}) copy-start(f32[64,768]{1,0:T(8,128)} %param.14) | copy-start | bytes 589828
  77.7 34.7 %copy-start.2 = (s32[64]{0:T(128)S(1)}, s32[64]{0:T(128)}, u32[]{:S(2)}) copy-start(s32[64]{0:T(128)} %param.15) | copy-start | bytes 772
  131.4 39.5 %copy-start = (f32[64,768]{1,0:T(8,128)S(1)}, f32[64,768]{1,0:T(8,128)}, u32[]{:S(2)}) copy-start(f32[64,768]{1,0:T(8,128)} %shard_map.113) | copy-start | bytes 589828

commit v2 on v1

v2 whole, which is shorter than its diff:
```python
import jax
import jax.numpy as jnp
from jax import lax
from jax.experimental import pallas as pl
from jax.experimental.pallas import tpu as pltpu
from jax.sharding import PartitionSpec as P

MESH = pl.DeviceIdType.MESH
F32 = jnp.float32
BF16 = jnp.bfloat16
D = 768
EPS = 1e-6
NEG = -1e30
SHARP = 1.0 / 0.07
VMEM_LIMIT = 56 * 1024 * 1024


class Place:
    def __init__(self):
        self.dp = lax.axis_index("dp")
        self.seq = lax.axis_index("seq")
        self.x_hi = self.dp // 4
        self.y = self.dp % 4
        self.z = self.seq // 4
        self.role = self.seq % 4
        self.x_lo = self.role // 2
        self.core = self.seq % 2
        self.k = self.seq // 2
        self.x = self.x_hi * 2 + self.x_lo
        self.m = self.dp * 4 + self.role


def send(src, dst, send_sem, recv_sem, dp, seq):
    pltpu.make_async_remote_copy(
        src_ref=src,
        dst_ref=dst,
        send_sem=send_sem,
        recv_sem=recv_sem,
        device_id=(dp, seq),
        device_id_type=MESH,
    ).start()


def drain(ref, sem):
    pltpu.make_async_copy(ref, ref, sem).wait()


def announce(me):
    sem = pltpu.get_barrier_semaphore()

    def slab(i, carry):
        to = lax.rem(me.k + i, 32) * 2 + me.core
        pl.semaphore_signal(sem, inc=1, device_id=(me.dp, to), device_id_type=MESH)
        return carry

    def plane(i, carry):
        to = lax.rem(me.m + i, 32)
        pl.semaphore_signal(
            sem, inc=1, device_id=(to // 4, me.z * 4 + to % 4), device_id_type=MESH
        )
        return carry

    lax.fori_loop(1, 32, slab, 0)
    lax.fori_loop(1, 32, plane, 0)


def arrive():
    pl.semaphore_wait(pltpu.get_barrier_semaphore(), 62)


def dot(a, b):
    return lax.dot_general(a, b, (((1,), (0,)), ((), ())), preferred_element_type=F32)


def dot_nt(a, b):
    return lax.dot_general(a, b, (((1,), (1,)), ((), ())), preferred_element_type=F32)


def dot_tn(a, b):
    return lax.dot_general(a, b, (((0,), (0,)), ((), ())), preferred_element_type=F32)


def iota(shape, dim):
    return lax.broadcasted_iota(jnp.int32, shape, dim)


def one_hot(condition):
    return jnp.where(condition, 1.0, 0.0).astype(BF16)


def gather_order(me):
    j = iota((1, D), 1)
    block, rest = j // 96, j % 96
    core, chunk, x_lo = block // 4, (block // 2) % 2, block % 2
    z8, r = rest // 12, rest % 12
    far = jnp.where(z8 == 0, 0, z8 + 4)
    near = jnp.where(z8 < 4, z8 + 1, z8 + 8)
    from_z = (me.z + jnp.where(chunk == 0, far, near)) % 16
    natural = (from_z * 4 + x_lo * 2 + core) * 12 + r
    return one_hot(iota((D, D), 0) == natural)


def scatter_order():
    j = iota((1, D), 1)
    dp, rest = j // 96, j % 96
    x_lo, z, r = rest // 48, (rest % 48) // 3, rest % 3
    natural = dp * 96 + z * 6 + x_lo * 3 + r
    return one_hot(iota((D, D), 0) == natural)


def split3(a):
    high = a.astype(BF16)
    rest = a - high.astype(F32)
    mid = rest.astype(BF16)
    low = (rest - mid.astype(F32)).astype(BF16)
    return jnp.concatenate([high.astype(F32), mid.astype(F32), low.astype(F32)], 0).astype(BF16)


def start_tokens(me, src, buf, local_sem, send_sem, recv_sem):
    pltpu.make_async_copy(src.at[me.k], buf.at[me.k], local_sem).start()

    def step(i, carry):
        j = 32 - i
        to = lax.rem(me.k + jnp.where(j % 2 == 0, 32 - j // 2, (j + 1) // 2), 32)
        send(src.at[to], buf.at[me.k], send_sem, recv_sem, me.dp, to * 2 + me.core)
        return carry

    lax.fori_loop(1, 32, step, 0)


def wait_tokens(me, src, buf, local_sem, recv_sem):
    pltpu.make_async_copy(src.at[me.k], buf.at[me.k], local_sem).wait()
    drain(buf.at[pl.ds(0, 31)], recv_sem)


def start_pair(me, buf, out, box, send_sem, recv_sem):
    rows = buf[...].astype(F32).reshape(256, D).astype(BF16)
    r, col = iota((128, 1), 0), iota((128, 256), 1)
    at = (r % 32) * 8 + r // 32
    theirs = dot(one_hot(col == at + 4 * (1 - me.core)), rows)
    box[...] = theirs.astype(BF16).reshape(4, 32, D)
    send(box, out.at[me.core], send_sem, recv_sem, me.dp, me.seq + 1 - 2 * me.core)
    mine = dot(one_hot(col == at + 4 * me.core), rows)
    out[me.core] = mine.astype(BF16).reshape(4, 32, D)


OFFSETS = (0, 5, 6, 7, 8, 9, 10, 11, 1, 2, 3, 4, 12, 13, 14, 15)


def start_weights(me, zbuf, send_sem, recv_z):
    for d in (8, 7, 9, 6, 10, 5, 11, 4, 12, 3, 13, 2, 14, 1, 15):
        j = OFFSETS.index(16 - d)
        to = lax.rem(me.z + d, 16) * 4 + me.role
        send(zbuf.at[0], zbuf.at[j], send_sem, recv_z.at[j // 8], me.dp, to)


def x_device(me, x):
    return (x // 2) * 4 + me.y, me.z * 4 + (x % 2) * 2 + me.core


def spread_first(me, zbuf, full, chunk, recv_z, send_sem, recv):
    drain(zbuf.at[pl.ds(0, 7 + chunk)], recv_z.at[chunk])
    r = iota((96, 1), 0)
    pick = one_hot(iota((96, 128), 1) == (r // 12) * 16 + r % 12)
    rows = zbuf[chunk * 8 : chunk * 8 + 8].reshape(128, 384)
    block = dot(pick, rows).astype(BF16)
    full[me.x_hi, me.y, me.core, chunk, me.x_lo] = block.reshape(2, 48, 384)
    a = full.at[me.x_hi, me.y, me.core, chunk, me.x_lo, 0]
    b = full.at[me.x_hi, me.y, me.core, chunk, me.x_lo, 1]
    for i in (2, 1, 3):
        send(a, a, send_sem, recv.at[chunk, 0], *x_device(me, lax.rem(me.x + i, 4)))
        send(b, b, send_sem, recv.at[chunk, 1], me.x_hi * 4 + lax.rem(me.y + i, 4), me.seq)


def spread_second(me, full, chunk, recv_first, send_sem, recv, send_pair, recv_pair):
    pair = me.seq + 1 - 2 * me.core
    drain(full.at[0, pl.ds(0, 3), 0, 0, 0, 0], recv_first.at[chunk, 0])
    a = full.at[:, me.y, me.core, chunk, :, 0]
    for n, i in enumerate((1, 3)):
        send(a, a, send_sem, recv.at[chunk, 0, n], me.x_hi * 4 + lax.rem(me.y + i, 4), me.seq)
    drain(full.at[0, pl.ds(0, 3), 0, 0, 0, 0], recv_first.at[chunk, 1])
    b = full.at[me.x_hi, :, me.core, chunk, me.x_lo, 1]
    for n, i in enumerate((1, 3)):
        send(b, b, send_sem, recv.at[chunk, 1, n], *x_device(me, lax.rem(me.x + i, 4)))
    send(a, a, send_pair, recv_pair, me.dp, pair)
    send(b, b, send_pair, recv_pair, me.dp, pair)


def spread_third(me, full, chunk, recv_second, send_sem, recv, send_pair, recv_pair):
    pair = me.seq + 1 - 2 * me.core
    for n, (i, o) in enumerate(((3, 1), (1, 3))):
        y, x = lax.rem(me.y + i, 4), lax.rem(me.x + i, 4)
        a = full.at[:, y, me.core, chunk, :, 0]
        drain(a, recv_second.at[chunk, 0, n])
        half = full.at[n, y, me.core, chunk, :, 0]
        send(half, half, send_sem, recv.at[chunk, 0, n], me.x_hi * 4 + lax.rem(me.y + o, 4), me.seq)
        b = full.at[x // 2, :, me.core, chunk, x % 2, 1]
        drain(b, recv_second.at[chunk, 1, n])
        half = full.at[x // 2, pl.ds(2 * n, 2), me.core, chunk, x % 2, 1]
        send(half, half, send_sem, recv.at[chunk, 1, n], *x_device(me, lax.rem(me.x + o, 4)))
        send(a, a, send_pair, recv_pair, me.dp, pair)
        send(b, b, send_pair, recv_pair, me.dp, pair)


def spread_last(me, full, chunk, recv_third, send_pair, recv_pair):
    pair = me.seq + 1 - 2 * me.core
    y, x = lax.rem(me.y + 2, 4), lax.rem(me.x + 2, 4)
    for n in range(2):
        a = full.at[n, y, me.core, chunk, :, 0]
        drain(a, recv_third.at[chunk, 0, n])
        send(a, a, send_pair, recv_pair, me.dp, pair)
        b = full.at[x // 2, pl.ds(2 * n, 2), me.core, chunk, x % 2, 1]
        drain(b, recv_third.at[chunk, 1, n])
        send(b, b, send_pair, recv_pair, me.dp, pair)


def start_pooled(me, part, box1, in1, send_sem, recv_sem):
    for q in range(4):
        box1[q] = part[2 * q : 2 * q + 2, :]
    in1[me.role] = box1[me.role]
    for i in range(1, 4):
        to = lax.rem(me.role + i, 4)
        send(box1.at[to], in1.at[me.role], send_sem, recv_sem, me.dp, me.z * 4 + to)


def pooled_along_z(me, in1, recv_first, buf2, send_sem, recv_sem):
    drain(in1.at[pl.ds(0, 3)], recv_first)
    buf2[me.z] = jnp.sum(in1[...], 0)

    def step(i, carry):
        j = 16 - i
        to = lax.rem(me.z + jnp.where(j % 2 == 0, 16 - j // 2, (j + 1) // 2), 16)
        send(buf2.at[me.z], buf2.at[me.z], send_sem, recv_sem, me.dp, to * 4 + me.role)
        return carry

    lax.fori_loop(1, 16, step, 0)


def pooled_in_plane(me, buf2, recv_second, pool, send_sem, recv_sem):
    drain(buf2.at[pl.ds(0, 15)], recv_second)
    pool[me.m] = jnp.sum(buf2[...], 0) * (1.0 / 2048.0)

    def step(i, carry):
        to = lax.rem(me.m + i, 32)
        send(pool.at[me.m], pool.at[me.m], send_sem, recv_sem, to // 4, me.z * 4 + to % 4)
        return carry

    lax.fori_loop(1, 32, step, 0)


def finish_pooled(pool, recv_sem, pooled):
    drain(pool.at[pl.ds(0, 31)], recv_sem)
    for m in range(32):
        pooled[2 * m : 2 * m + 2, :] = pool[m]


def start_weight_sum(me, box, pair_buf, send_sem, recv_sem):
    send(
        box.at[1 - me.core], pair_buf, send_sem, recv_sem, me.dp, me.seq + 1 - 2 * me.core
    )


def plane_weight_sum(me, box, pair_buf, recv_pair, own, buf, send_sem, recv_sem):
    drain(pair_buf, recv_pair)
    own[...] = (box[me.core].astype(F32) + pair_buf[...].astype(F32)).astype(BF16)
    n = me.dp * 2 + me.x_lo
    buf[n] = own[n]

    def step(i, carry):
        to = lax.rem(n + i, 16)
        send(
            own.at[to], buf.at[n], send_sem, recv_sem,
            to // 2, me.z * 4 + (to % 2) * 2 + me.core,
        )
        return carry

    lax.fori_loop(1, 16, step, 0)


def second_weight_sum(me, buf, recv_sem, box_z, buf_z, send_sem, recv_z):
    drain(buf.at[pl.ds(0, 15)], recv_sem)
    total = lax.fori_loop(
        0, 16, lambda i, t: t + buf[i].astype(F32), jnp.zeros((48, 384), F32)
    )
    box_z[...] = jnp.zeros_like(box_z)
    for z in range(16):
        box_z[z, 0:3, :] = total[3 * z : 3 * z + 3, :]
    buf_z[me.z] = box_z[me.z]

    def step(i, carry):
        to = lax.rem(me.z + i, 16)
        send(box_z.at[to], buf_z.at[me.z], send_sem, recv_z, me.dp, to * 4 + me.role)
        return carry

    lax.fori_loop(1, 16, step, 0)


def third_weight_sum(me, buf_z, recv_z, rows, send_sem, recv_sem):
    drain(buf_z.at[pl.ds(0, 15)], recv_z)
    rows[me.core] = jnp.sum(buf_z[...], 0)
    send(
        rows.at[me.core], rows.at[me.core], send_sem, recv_sem,
        me.dp, me.seq + 1 - 2 * me.core,
    )


def finish_weight_sum(me, rows, recv_sem, out):
    drain(rows.at[0], recv_sem)
    left, right = rows[0], rows[1]
    first = me.core == 0
    out[0:1, 0:384] = jnp.where(first, left[0:1], right[1:2])
    out[0:1, 384:768] = jnp.where(first, right[0:1], left[2:3])
    out[0:1, 768:1152] = jnp.where(first, left[1:2], right[2:3])


def start_back_pair(me, grads, buf, send_sem, recv_sem):
    theirs = 1 - me.core
    send(grads.at[theirs], buf.at[me.core], send_sem, recv_sem, me.dp, me.seq + 1 - 2 * me.core)
    buf[me.core] = grads[me.core]


def start_back(me, buf, recv_pair, box, out, local_sem, send_sem, recv_sem):
    drain(buf.at[0], recv_pair)
    r = iota((256, 1), 0)
    at = ((r // 4) % 2) * 128 + (r % 4) * 32 + r // 8
    rows = dot(one_hot(iota((256, 256), 1) == at), buf[...].reshape(256, D))
    box[...] = rows.reshape(32, 8, D).astype(BF16)
    start_tokens(me, box, out, local_sem, send_sem, recv_sem)


def normalize(x):
    centered = x - jnp.mean(x, -1, keepdims=True)
    inverse = lax.rsqrt(jnp.mean(centered * centered, -1, keepdims=True) + EPS)
    return centered * inverse, inverse


def exact(a, b, contract):
    return lax.dot_general(
        a, b, (contract, ((), ())), precision=lax.Precision.HIGHEST, preferred_element_type=F32
    )


def window_units(windows, out):
    w = windows[...]
    out[...] = w * lax.rsqrt(jnp.mean(w * w, -1, keepdims=True) + EPS) * D ** (-0.5)


def contrast(pooled, units, positives, loss, grad):
    p, root = pooled[...], D ** (-0.5)
    inverse = lax.rsqrt(jnp.mean(p * p, -1, keepdims=True) + EPS)
    logits = exact(units[...], p * inverse * root, ((1,), (1,))) * SHARP
    matched = iota((64, 64), 0) == positives[...].reshape(1, 64)
    total = -jnp.sum(jnp.where(matched, logits, 0.0))
    slope = jnp.where(matched, -1.0, 0.0)
    for axis in range(2):
        top = jnp.max(logits, axis, keepdims=True)
        weight = jnp.exp(logits - top)
        size = jnp.sum(weight, axis, keepdims=True)
        total = total + 0.5 * jnp.sum(top + jnp.log(size))
        slope = slope + 0.5 * (weight / size)
    loss[...] = jnp.full((1, 1), total * (1.0 / 64.0), F32)
    grad_unit = exact(slope * (SHARP / 64.0), units[...], ((0,), (0,)))
    inner = jnp.mean(grad_unit * p, -1, keepdims=True)
    grad[...] = inverse * root * (grad_unit - p * (inverse * inverse) * inner)


def clip_pick():
    return one_hot((iota((8, 256), 1) % 32) // 4 == iota((8, 256), 0))


def unit_rows(ref, u, columns):
    return jnp.concatenate(
        [ref[u * 64 : u * 64 + 64, columns], ref[128 + u * 64 : 192 + u * 64, columns]], 0
    )


def put_rows(ref, u, columns, value):
    ref[u * 64 : u * 64 + 64, columns] = value[:64]
    ref[128 + u * 64 : 192 + u * 64, columns] = value[64:]


def heads(a):
    even = iota(a.shape, 1) < 64
    zero = jnp.zeros_like(a)
    return jnp.concatenate([jnp.where(even, a, zero), jnp.where(even, zero, a)], 0)


def same_patch():
    return (iota((256, 128), 0) // 32) % 2 == (iota((256, 128), 1) // 32) % 2


def norm_tokens(tokens, scale, bias, order, normed):
    unit, _ = normalize(tokens[...].reshape(256, D).astype(F32))
    rows = (unit * scale[...].reshape(1, D) + bias[...].reshape(1, D)).astype(BF16)
    normed[...] = dot(rows, order[...]).astype(BF16)


def project(normed, full, qkv):
    for n in range(6):
        weight = full[n // 4, n % 4].reshape(D, 384)
        qkv[:, n * 384 : n * 384 + 384] = dot(normed[...], weight).astype(BF16)


def attend(qkv, prob, context):
    keep = same_patch()
    for j in range(6):
        for u in range(2):
            columns = [slice(s * D + j * 128, s * D + j * 128 + 128) for s in range(3)]
            query, key, value = [unit_rows(qkv, u, c) for c in columns]
            score = dot_nt(heads(query), key) * 0.125
            score = jnp.where(keep, score, NEG)
            top = jnp.max(score, -1, keepdims=True)
            weight = jnp.exp(score - top)
            p = weight / jnp.sum(weight, -1, keepdims=True)
            prob[j * 2 + u] = p
            half = p.astype(BF16)
            both = jnp.concatenate([half[:128], half[128:]], 1)
            mixed = dot(both, heads(value)).astype(BF16)
            put_rows(context, u, slice(j * 128, j * 128 + 128), mixed)


def pool_clips(tokens, context, order, full, part):
    pick = clip_pick()
    ctx_sum = split3(dot(pick, context[...]))
    ctx_sum = dot(ctx_sum, order[...]).astype(BF16)
    sums = dot(pick, tokens[...].reshape(256, D))
    for n in range(2):
        weight = full[1, 2 + n].reshape(D, 384)
        s = dot(ctx_sum, weight)
        columns = slice(n * 384, n * 384 + 384)
        part[:, columns] = sums[:, columns] + s[0:8] + s[8:16] + s[16:24]


def spread(upstream, grad_clip):
    pick = one_hot((iota((256, 24), 0) % 32) // 4 == iota((256, 24), 1) % 8)
    return upstream[...].reshape(256, D).astype(F32) + dot(pick, split3(grad_clip))


def project_back(grad_half, full, order, grad_context):
    back = dot_nt(grad_half[:, :384], full[1, 2].reshape(D, 384))
    back = back + dot_nt(grad_half[:, 384:], full[1, 3].reshape(D, 384))
    grad_context[...] = dot_nt(back.astype(BF16), order[...]).astype(BF16)


def weight_term(grad_half, scatter, context, box):
    ordered = dot(context[...], scatter[...]).astype(BF16)
    term = dot_tn(ordered, grad_half).astype(BF16)
    for n in range(16):
        for c in range(2):
            box[c, n] = term[n * 48 : n * 48 + 48, c * 384 : c * 384 + 384]


def backward_attention(pairs, qkv, prob, grad_context, grad_qkv):
    for j in pairs:
        for u in range(2):
            columns = [slice(s * D + j * 128, s * D + j * 128 + 128) for s in range(3)]
            query, key, value = [unit_rows(qkv, u, c) for c in columns]
            grad = heads(unit_rows(grad_context, u, slice(j * 128, j * 128 + 128)))
            p = prob[j * 2 + u]
            half = p.astype(BF16)
            grad_prob = dot_nt(grad, value)
            grad_value = dot_tn(half, grad).astype(BF16)
            row = jnp.sum(p * grad_prob, -1, keepdims=True)
            grad_score = (p * (grad_prob - row) * 0.125).astype(BF16)
            both = jnp.concatenate([grad_score[:128], grad_score[128:]], 1)
            put_rows(grad_qkv, u, columns[0], dot(both, heads(key)).astype(BF16))
            put_rows(grad_qkv, u, columns[1], dot_tn(grad_score, heads(query)).astype(BF16))
            put_rows(grad_qkv, u, columns[2], grad_value)


def backward_tokens(tokens, grad_output, grad_qkv, full, order, scale, out):
    back = jnp.zeros((256, D), F32)
    for n in range(6):
        weight = full[n // 4, n % 4].reshape(D, 384)
        back = back + dot_nt(grad_qkv[:, n * 384 : n * 384 + 384], weight)
    grad_normed = dot_nt(back.astype(BF16), order[...])
    scaled = grad_normed * scale[...].reshape(1, D)
    unit, inverse = normalize(tokens[...].reshape(256, D).astype(F32))
    grad_norm = inverse * (
        scaled
        - jnp.mean(scaled, -1, keepdims=True)
        - unit * jnp.mean(scaled * unit, -1, keepdims=True)
    )
    out[...] = (grad_output + grad_norm).astype(BF16).reshape(2, 4, 32, D)


def kernel(
    video, upstream, w_qkv, w_out, scale_in, bias_in, windows_in, positives_in,
    video_out, weight_out, pooled_out, loss_out,
    wq, wo, scale, bias, windows, positives, order, scatter,
    vbuf, ubuf, vbox, ubox, tokens, ups, zbuf, full, normed, qkv, prob, context, part,
    box1, in1, buf2, pool, pooled, units, grad_pooled, grad_output, grad_context, grad_qkv, grads,
    box, gw_pair, gw_own, gw_buf, box_z, buf_z, rows, pair_buf, out_box,
    load, local, tok_send, tok_recv, pair_send, pair_recv,
    w_send, recv_z, recv_first, recv_second, recv_third, wp_sem,
    pool_send, pool_recv, gw_send, gw_recv, out_send, out_recv, store,
):
    me = Place()
    loads = [(w_qkv, wq), (w_out, wo), (scale_in, scale), (bias_in, bias)]
    loads += [(windows_in, windows), (positives_in, positives)]
    loads = [pltpu.make_async_copy(a, b, load.at[i]) for i, (a, b) in enumerate(loads)]
    for copy in loads:
        copy.start()
    announce(me)
    loads[0].wait()
    loads[1].wait()
    column = pl.multiple_of(lax.rem(me.dp, 6) * 384, 384)
    column_out = pl.multiple_of(lax.rem(me.dp, 2) * 384, 384)
    piece = jnp.where(me.dp < 6, wq[:, pl.ds(column, 384)], wo[:, pl.ds(column_out, 384)])
    zbuf[0] = jnp.concatenate([piece.astype(F32), jnp.zeros((4, 384), F32)], 0).astype(BF16)
    arrive()
    start_weights(me, zbuf, w_send.at[0], recv_z)
    start_tokens(me, video, vbuf, local.at[0], tok_send.at[0], tok_recv.at[0])
    order[...] = gather_order(me)
    scatter[...] = scatter_order()
    for copy in loads[2:]:
        copy.wait()
    window_units(windows, units)
    for chunk in range(2):
        spread_first(me, zbuf, full, chunk, recv_z, w_send.at[1], recv_first)
    pair_sems = (wp_sem.at[0], wp_sem.at[1])
    for chunk in range(2):
        spread_second(me, full, chunk, recv_first, w_send.at[2], recv_second, *pair_sems)
    for chunk in range(2):
        spread_third(me, full, chunk, recv_second, w_send.at[3], recv_third, *pair_sems)
    wait_tokens(me, video, vbuf, local.at[0], tok_recv.at[0])
    start_pair(me, vbuf, tokens, vbox, pair_send.at[0], pair_recv.at[0])
    start_tokens(me, upstream, ubuf, local.at[1], tok_send.at[1], tok_recv.at[1])
    for chunk in range(2):
        spread_last(me, full, chunk, recv_third, *pair_sems)
    drain(tokens.at[0], pair_recv.at[0])
    norm_tokens(tokens, scale, bias, order, normed)
    drain(full.at[:, :, 0], wp_sem.at[1])
    project(normed, full, qkv)
    attend(qkv, prob, context)
    pool_clips(tokens, context, order, full, part)
    start_pooled(me, part, box1, in1, pool_send.at[0], pool_recv.at[0])
    pooled_along_z(me, in1, pool_recv.at[0], buf2, pool_send.at[1], pool_recv.at[1])
    wait_tokens(me, upstream, ubuf, local.at[1], tok_recv.at[1])
    start_pair(me, ubuf, ups, ubox, pair_send.at[1], pair_recv.at[1])
    pooled_in_plane(me, buf2, pool_recv.at[1], pool, pool_send.at[2], pool_recv.at[2])
    drain(ups.at[0], pair_recv.at[1])
    finish_pooled(pool, pool_recv.at[2], pooled)
    contrast(pooled, units, positives, loss_out, grad_pooled)
    save = pltpu.make_async_copy(pooled, pooled_out, store)
    save.start()
    grad_clip = grad_pooled[pl.ds(pl.multiple_of(me.dp * 8, 8), 8), :] * 64.0
    grad_output[...] = spread(ups, grad_clip)
    grad_half = grad_output[...].astype(BF16)
    weight_term(grad_half, scatter, context, box)
    start_weight_sum(me, box, gw_pair, gw_send.at[0], gw_recv.at[0])
    project_back(grad_half, full, order, grad_context)
    backward_attention((0, 1), qkv, prob, grad_context, grad_qkv)
    plane_weight_sum(
        me, box, gw_pair, gw_recv.at[0], gw_own, gw_buf, gw_send.at[1], gw_recv.at[1]
    )
    backward_attention((2, 3, 4, 5), qkv, prob, grad_context, grad_qkv)
    backward_tokens(tokens, grad_output[...], grad_qkv, full, order, scale, grads)
    start_back_pair(me, grads, pair_buf, out_send.at[0], out_recv.at[0])
    start_back(
        me, pair_buf, out_recv.at[0], out_box, video_out, local.at[2], out_send.at[1], out_recv.at[1]
    )
    second_weight_sum(me, gw_buf, gw_recv.at[1], box_z, buf_z, gw_send.at[2], gw_recv.at[2])
    third_weight_sum(me, buf_z, gw_recv.at[2], rows, gw_send.at[3], gw_recv.at[3])
    finish_weight_sum(me, rows, gw_recv.at[3], weight_out)
    wait_tokens(me, out_box, video_out, local.at[2], out_recv.at[1])
    save.wait()
    drain(zbuf.at[pl.ds(0, 15)], w_send.at[0])
    drain(full.at[0, pl.ds(0, 3), 0, 0], w_send.at[1])
    drain(full.at[0, pl.ds(0, 2)], w_send.at[2])
    drain(full.at[0, 0], w_send.at[3])
    drain(full.at[:, :, 0], wp_sem.at[0])
    for i in range(2):
        drain(vbuf.at[pl.ds(0, 31)], tok_send.at[i])
        drain(vbox, pair_send.at[i])
    drain(in1.at[pl.ds(0, 3)], pool_send.at[0])
    drain(buf2.at[pl.ds(0, 15)], pool_send.at[1])
    drain(pool.at[pl.ds(0, 31)], pool_send.at[2])
    drain(gw_pair, gw_send.at[0])
    drain(gw_buf.at[pl.ds(0, 15)], gw_send.at[1])
    drain(buf_z.at[pl.ds(0, 15)], gw_send.at[2])
    drain(rows.at[0], gw_send.at[3])
    drain(pair_buf.at[0], out_send.at[0])
    drain(out_box.at[pl.ds(0, 31)], out_send.at[1])


def shape(*dims, dtype=BF16):
    return jax.ShapeDtypeStruct(dims, dtype)


def scratch_shapes():
    dma = pltpu.SemaphoreType.DMA

    def half(*dims):
        return pltpu.VMEM(dims, BF16)

    def single(*dims):
        return pltpu.VMEM(dims, F32)

    return [
        half(12, 3 * D), half(12, D), single(D), single(D), single(64, D),
        pltpu.VMEM((64,), jnp.int32), half(D, D), half(D, D),
        half(32, 8, D), half(32, 8, D), half(4, 32, D), half(4, 32, D),
        half(2, 4, 32, D), half(2, 4, 32, D), half(16, 16, 384), half(2, 4, 2, 2, 2, 2, 48, 384),
        half(256, D), half(256, 3 * D), single(12, 256, 128), half(256, D), single(8, D),
        single(4, 2, D), single(4, 2, D), single(16, 2, D), single(32, 2, D),
        single(64, D), single(64, D), single(64, D), single(256, D),
        half(256, D), half(256, 3 * D), half(2, 4, 32, D),
        half(2, 16, 48, 384), half(16, 48, 384), half(16, 48, 384), half(16, 48, 384),
        single(16, 4, 384), single(16, 4, 384), single(2, 4, 384),
        half(2, 4, 32, D), half(32, 8, D),
        dma((6,)), dma((3,)), dma((2,)), dma((2,)), dma((2,)), dma((2,)),
        dma((4,)), dma((2,)), dma((2, 2)), dma((2, 2, 2)), dma((2, 2, 2)), dma((2,)),
        dma((3,)), dma((3,)), dma((4,)), dma((4,)), dma((2,)), dma((2,)), dma,
    ]


def per_device(video, upstream, standardize_scale, ln_bias, w_qkv, w_out, windows, positives):
    anywhere, vmem = pl.BlockSpec(memory_space=pl.ANY), pl.BlockSpec(memory_space=pltpu.VMEM)
    grad_video, grad_out_weight, pooled, loss = pl.pallas_call(
        kernel,
        out_shape=[
            shape(32, 8, D), shape(1, 1152, dtype=F32), shape(64, D, dtype=F32),
            shape(1, 1, dtype=F32),
        ],
        in_specs=[anywhere] * 8,
        out_specs=[anywhere, vmem, anywhere, vmem],
        scratch_shapes=scratch_shapes(),
        compiler_params=pltpu.CompilerParams(
            vmem_limit_bytes=VMEM_LIMIT, collective_id=1, has_side_effects=True
        ),
    )(
        video.reshape(32, 8, D), upstream.reshape(32, 8, D), w_qkv, w_out,
        standardize_scale, ln_bias, windows, positives,
    )
    return grad_video.reshape(1, 1, 256, D), grad_out_weight, pooled, loss.reshape(())


def solution(mesh):
    in_specs = (
        P("dp", "seq", None, None),
        P("dp", "seq", None, None),
        P(),
        P(),
        P("seq", None),
        P("seq", None),
        P(),
        P(),
    )
    out_specs = (P("dp", "seq", None, None), P(("dp", "seq"), None), P(), P())
    return jax.shard_map(
        per_device, mesh=mesh, in_specs=in_specs, out_specs=out_specs, check_vma=False
    )
```

time: 175 us -> 122 us (0.70); the launches traced: 173 us -> 122 us
  Pallas kernels: 150 us -> 116 us
  other arithmetic: 9.15 us -> 0 us
  local copies, waits for them, and re-layouts: 7.05 us -> 3.08 us
  matrix products: 2.86 us -> 0 us
    pallas_call x5 -> x1, Pallas kernels: 150 us -> 116 us  [per_device(): pl.pallas_call(kernel, out_shape=[shape(32, 8, D), shape(1, 1152, dtype=F...]
    reduce_sum x5 -> x0, other arithmetic: 3.99 us -> none  [the longest x3 1.9 us: contrast(): return 0.5 * (jnp.mean(row_lse) + jnp.mean(column_lse)) - jnp.mean(positive)]
    convert_element_type x2 -> x0, other arithmetic: 2.91 us -> none  [one_hot(): return jnp.where(condition, 1.0, 0.0).astype(BF16)]
    dot_general x2 -> x0, matrix products: 2.86 us -> none  [contrast(): jnp.dot(clip_unit, window_unit.T, precision=lax.Precision.HIGHEST) * SHARP]
    reshape x2 -> x0, local copies, waits for them, and re-layouts: 2.55 us -> none  [per_device(): scale, bias = (standardize_scale.reshape(1, D), ln_bias.reshape(1, D))]
    unnamed x9 -> x7, local copies, waits for them, and re-layouts: 3.74 us -> 3.08 us
where the time goes in v2:
time: 122 us
  Pallas kernels  116 us (95%)
  local copies, waits for them, and re-layouts  3.08 us (3%)
  between operations  2.41 us (2%)
    pallas_call x1, Pallas kernels, per_device(): pl.pallas_call(kernel, out_shape=[shape(32, 8, D), shape(1, 1152, dtype=F...  116 us
    unnamed x7, local copies, waits for them, and re-layouts  3.08 us

profile of v2, /device:TPU:1, one launch (start us, length us, event | category | flops | bytes accessed | tf_op | source)
XLA Modules:
  0.0 121.7 jit_solution(2215518797189621119)
XLA Ops:
  0.6 116.2 %shard_map.111 = (bf16[32,8,768]{2,1,0:T(8,128)(2,1)}, f32[1,1152]{1,0:T(1,128)}, f32[64,768]{1,0:T(8,128)}, f32[1,1]{1,0:T(1,128)}) custom-call(bf16[32,8,768]{2,1,0:T(8,128)(2,1)} %bitcast.5, bf16[32,8,768]{2,1,0:T(8,128)(2,1)} %bitcast.6, bf16[12,2304]{1,0:T(8,128)(2,1)} %w_qkv.1, bf16[12,768]{1,0:T(8,128)(2,1)} %w_out.1, f32[768]{0:T(1024)} %scale_in.1, ...), custom_call_target="tpu_custom_call" | custom-call | tf_op jit(solution)/shard_map/pallas_call | solution.py:620
  116.8 0.0 copy-start.1
  116.8 0.0 copy-start
  116.9 1.8 %copy.16 = bf16[1,1,256,768]{3,2,1,0:T(8,128)(2,1)} copy(bf16[1,1,256,768]{3,2,1,0:T(8,128)(2,1)} %bitcast.4) | data formatting | bytes 786432
  118.7 0.0 copy-done.1
  118.7 0.6 copy.17
  119.3 0.0 copy-done
  119.3 0.7 copy.18
Async XLA Ops:
  116.8 1.8 %copy-start.1 = (f32[1,1152]{1,0:T(1,128)S(1)}, f32[1,1152]{1,0:T(1,128)}, u32[]{:S(2)}) copy-start(f32[1,1152]{1,0:T(1,128)} %get-tuple-element.17) | copy-start | bytes 13828
  116.8 2.4 %copy-start = (f32[64,768]{1,0:T(8,128)S(1)}, f32[64,768]{1,0:T(8,128)}, u32[]{:S(2)}) copy-start(f32[64,768]{1,0:T(8,128)} %get-tuple-element.18) | copy-start | bytes 589828

commit v3 on v2

--- a/solution.py
+++ b/solution.py
@@ -41,6 +41,10 @@
     ).start()
 
 
+def wrap(a, n):
+    return jnp.where(a >= n, a - n, a)
+
+
 def drain(ref, sem):
     pltpu.make_async_copy(ref, ref, sem).wait()
 
@@ -49,19 +53,21 @@
     sem = pltpu.get_barrier_semaphore()
 
     def slab(i, carry):
-        to = lax.rem(me.k + i, 32) * 2 + me.core
+        to = wrap(me.k + i, 32) * 2 + me.core
         pl.semaphore_signal(sem, inc=1, device_id=(me.dp, to), device_id_type=MESH)
         return carry
 
     def plane(i, carry):
-        to = lax.rem(me.m + i, 32)
-        pl.semaphore_signal(
-            sem, inc=1, device_id=(to // 4, me.z * 4 + to % 4), device_id_type=MESH
-        )
+        dp = wrap(me.dp + i, 8)
+        for role in range(4):
+            pl.semaphore_signal(sem, inc=1, device_id=(dp, me.z * 4 + role), device_id_type=MESH)
         return carry
 
     lax.fori_loop(1, 32, slab, 0)
-    lax.fori_loop(1, 32, plane, 0)
+    lax.fori_loop(1, 8, plane, 0)
+    for i in range(1, 4):
+        to = me.z * 4 + wrap(me.role + i, 4)
+        pl.semaphore_signal(sem, inc=1, device_id=(me.dp, to), device_id_type=MESH)
 
 
 def arrive():
@@ -93,9 +99,8 @@
     block, rest = j // 96, j % 96
     core, chunk, x_lo = block // 4, (block // 2) % 2, block % 2
     z8, r = rest // 12, rest % 12
-    far = jnp.where(z8 == 0, 0, z8 + 4)
-    near = jnp.where(z8 < 4, z8 + 1, z8 + 8)
-    from_z = (me.z + jnp.where(chunk == 0, far, near)) % 16
+    near = jnp.where(z8 < 5, z8, z8 + 8)
+    from_z = (me.z + jnp.where(chunk == 0, near, z8 + 5)) % 16
     natural = (from_z * 4 + x_lo * 2 + core) * 12 + r
     return one_hot(iota((D, D), 0) == natural)
 
@@ -116,16 +121,19 @@
     return jnp.concatenate([high.astype(F32), mid.astype(F32), low.astype(F32)], 0).astype(BF16)
 
 
-def start_tokens(me, src, buf, local_sem, send_sem, recv_sem):
-    pltpu.make_async_copy(src.at[me.k], buf.at[me.k], local_sem).start()
+def start_tokens(me, src, buf, local_sem, send_sem, recv_sem, far=16, near=1):
+    def one(to):
+        send(src.at[to], buf.at[me.k], send_sem, recv_sem, me.dp, to * 2 + me.core)
 
     def step(i, carry):
-        j = 32 - i
-        to = lax.rem(me.k + jnp.where(j % 2 == 0, 32 - j // 2, (j + 1) // 2), 32)
-        send(src.at[to], buf.at[me.k], send_sem, recv_sem, me.dp, to * 2 + me.core)
+        one(wrap(me.k + 16 - i, 32))
+        one(wrap(me.k + 16 + i, 32))
         return carry
 
-    lax.fori_loop(1, 32, step, 0)
+    if far == 16:
+        pltpu.make_async_copy(src.at[me.k], buf.at[me.k], local_sem).start()
+        one(wrap(me.k + 16, 32))
+    lax.fori_loop(max(16 - far, 1), 17 - near, step, 0)
 
 
 def wait_tokens(me, src, buf, local_sem, recv_sem):
@@ -144,13 +152,13 @@
     out[me.core] = mine.astype(BF16).reshape(4, 32, D)
 
 
-OFFSETS = (0, 5, 6, 7, 8, 9, 10, 11, 1, 2, 3, 4, 12, 13, 14, 15)
+OFFSETS = (0, 1, 2, 3, 4, 13, 14, 15, 5, 6, 7, 8, 9, 10, 11, 12)
 
 
 def start_weights(me, zbuf, send_sem, recv_z):
-    for d in (8, 7, 9, 6, 10, 5, 11, 4, 12, 3, 13, 2, 14, 1, 15):
+    for d in (12, 13, 3, 14, 2, 15, 1, 8, 7, 9, 6, 10, 5, 11, 4):
         j = OFFSETS.index(16 - d)
-        to = lax.rem(me.z + d, 16) * 4 + me.role
+        to = wrap(me.z + d, 16) * 4 + me.role
         send(zbuf.at[0], zbuf.at[j], send_sem, recv_z.at[j // 8], me.dp, to)
 
 
@@ -168,20 +176,20 @@
     a = full.at[me.x_hi, me.y, me.core, chunk, me.x_lo, 0]
     b = full.at[me.x_hi, me.y, me.core, chunk, me.x_lo, 1]
     for i in (2, 1, 3):
-        send(a, a, send_sem, recv.at[chunk, 0], *x_device(me, lax.rem(me.x + i, 4)))
-        send(b, b, send_sem, recv.at[chunk, 1], me.x_hi * 4 + lax.rem(me.y + i, 4), me.seq)
-
-
-def spread_second(me, full, chunk, recv_first, send_sem, recv, send_pair, recv_pair):
+        send(a, a, send_sem, recv.at[chunk, 0], *x_device(me, wrap(me.x + i, 4)))
+        send(b, b, send_sem, recv.at[chunk, 1], me.x_hi * 4 + wrap(me.y + i, 4), me.seq)
+
+
+def spread_second(me, full, chunk, recv_first, send_sem, recv, send_pair, recv_pair, to=(1, 3)):
     pair = me.seq + 1 - 2 * me.core
     drain(full.at[0, pl.ds(0, 3), 0, 0, 0, 0], recv_first.at[chunk, 0])
     a = full.at[:, me.y, me.core, chunk, :, 0]
-    for n, i in enumerate((1, 3)):
-        send(a, a, send_sem, recv.at[chunk, 0, n], me.x_hi * 4 + lax.rem(me.y + i, 4), me.seq)
+    for i in to:
+        send(a, a, send_sem, recv.at[chunk, 0, i - 1], me.x_hi * 4 + wrap(me.y + i, 4), me.seq)
     drain(full.at[0, pl.ds(0, 3), 0, 0, 0, 0], recv_first.at[chunk, 1])
     b = full.at[me.x_hi, :, me.core, chunk, me.x_lo, 1]
-    for n, i in enumerate((1, 3)):
-        send(b, b, send_sem, recv.at[chunk, 1, n], *x_device(me, lax.rem(me.x + i, 4)))
+    for i in to:
+        send(b, b, send_sem, recv.at[chunk, 1, i - 1], *x_device(me, wrap(me.x + i, 4)))
     send(a, a, send_pair, recv_pair, me.dp, pair)
     send(b, b, send_pair, recv_pair, me.dp, pair)
 
@@ -189,22 +197,22 @@
 def spread_third(me, full, chunk, recv_second, send_sem, recv, send_pair, recv_pair):
     pair = me.seq + 1 - 2 * me.core
     for n, (i, o) in enumerate(((3, 1), (1, 3))):
-        y, x = lax.rem(me.y + i, 4), lax.rem(me.x + i, 4)
+        y, x = wrap(me.y + i, 4), wrap(me.x + i, 4)
         a = full.at[:, y, me.core, chunk, :, 0]
-        drain(a, recv_second.at[chunk, 0, n])
+        drain(a, recv_second.at[chunk, 0, 2 * n])
         half = full.at[n, y, me.core, chunk, :, 0]
-        send(half, half, send_sem, recv.at[chunk, 0, n], me.x_hi * 4 + lax.rem(me.y + o, 4), me.seq)
+        send(half, half, send_sem, recv.at[chunk, 0, n], me.x_hi * 4 + wrap(me.y + o, 4), me.seq)
         b = full.at[x // 2, :, me.core, chunk, x % 2, 1]
-        drain(b, recv_second.at[chunk, 1, n])
+        drain(b, recv_second.at[chunk, 1, 2 * n])
         half = full.at[x // 2, pl.ds(2 * n, 2), me.core, chunk, x % 2, 1]
-        send(half, half, send_sem, recv.at[chunk, 1, n], *x_device(me, lax.rem(me.x + o, 4)))
+        send(half, half, send_sem, recv.at[chunk, 1, n], *x_device(me, wrap(me.x + o, 4)))
         send(a, a, send_pair, recv_pair, me.dp, pair)
         send(b, b, send_pair, recv_pair, me.dp, pair)
 
 
 def spread_last(me, full, chunk, recv_third, send_pair, recv_pair):
     pair = me.seq + 1 - 2 * me.core
-    y, x = lax.rem(me.y + 2, 4), lax.rem(me.x + 2, 4)
+    y, x = wrap(me.y + 2, 4), wrap(me.x + 2, 4)
     for n in range(2):
         a = full.at[n, y, me.core, chunk, :, 0]
         drain(a, recv_third.at[chunk, 0, n])
@@ -214,12 +222,24 @@
         send(b, b, send_pair, recv_pair, me.dp, pair)
 
 
+def spread_direct(me, full, chunk, recv_second, send_pair, recv_pair):
+    pair = me.seq + 1 - 2 * me.core
+    for i in (1, 3, 2):
+        a = full.at[:, wrap(me.y + 4 - i, 4), me.core, chunk, :, 0]
+        drain(a, recv_second.at[chunk, 0, i - 1])
+        send(a, a, send_pair, recv_pair, me.dp, pair)
+        x = wrap(me.x + 4 - i, 4)
+        b = full.at[x // 2, :, me.core, chunk, x % 2, 1]
+        drain(b, recv_second.at[chunk, 1, i - 1])
+        send(b, b, send_pair, recv_pair, me.dp, pair)
+
+
 def start_pooled(me, part, box1, in1, send_sem, recv_sem):
     for q in range(4):
         box1[q] = part[2 * q : 2 * q + 2, :]
     in1[me.role] = box1[me.role]
     for i in range(1, 4):
-        to = lax.rem(me.role + i, 4)
+        to = wrap(me.role + i, 4)
         send(box1.at[to], in1.at[me.role], send_sem, recv_sem, me.dp, me.z * 4 + to)
 
 
@@ -227,25 +247,26 @@
     drain(in1.at[pl.ds(0, 3)], recv_first)
     buf2[me.z] = jnp.sum(in1[...], 0)
 
-    def step(i, carry):
-        j = 16 - i
-        to = lax.rem(me.z + jnp.where(j % 2 == 0, 16 - j // 2, (j + 1) // 2), 16)
-        send(buf2.at[me.z], buf2.at[me.z], send_sem, recv_sem, me.dp, to * 4 + me.role)
-        return carry
-
-    lax.fori_loop(1, 16, step, 0)
+    for i in (8, 9, 7, 10, 6, 11, 5, 12, 4, 13, 3, 14, 2, 15, 1):
+        to = wrap(me.z + i, 16) * 4 + me.role
+        send(buf2.at[me.z], buf2.at[me.z], send_sem, recv_sem, me.dp, to)
 
 
 def pooled_in_plane(me, buf2, recv_second, pool, send_sem, recv_sem):
     drain(buf2.at[pl.ds(0, 15)], recv_second)
     pool[me.m] = jnp.sum(buf2[...], 0) * (1.0 / 2048.0)
 
+    mine = pool.at[me.m]
+
     def step(i, carry):
-        to = lax.rem(me.m + i, 32)
-        send(pool.at[me.m], pool.at[me.m], send_sem, recv_sem, to // 4, me.z * 4 + to % 4)
+        dp = wrap(me.dp + i, 8)
+        for role in range(4):
+            send(mine, mine, send_sem, recv_sem, dp, me.z * 4 + role)
         return carry
 
-    lax.fori_loop(1, 32, step, 0)
+    lax.fori_loop(1, 8, step, 0)
+    for i in range(1, 4):
+        send(mine, mine, send_sem, recv_sem, me.dp, me.z * 4 + wrap(me.role + i, 4))
 
 
 def finish_pooled(pool, recv_sem, pooled):
@@ -267,14 +288,16 @@
     buf[n] = own[n]
 
     def step(i, carry):
-        to = lax.rem(n + i, 16)
-        send(
-            own.at[to], buf.at[n], send_sem, recv_sem,
-            to // 2, me.z * 4 + (to % 2) * 2 + me.core,
-        )
+        dp = wrap(me.dp + i, 8)
+        for x_lo in range(2):
+            to = me.z * 4 + x_lo * 2 + me.core
+            send(own.at[dp * 2 + x_lo], buf.at[n], send_sem, recv_sem, dp, to)
         return carry
 
-    lax.fori_loop(1, 16, step, 0)
+    lax.fori_loop(1, 8, step, 0)
+    other = 1 - me.x_lo
+    to = me.z * 4 + other * 2 + me.core
+    send(own.at[me.dp * 2 + other], buf.at[n], send_sem, recv_sem, me.dp, to)
 
 
 def second_weight_sum(me, buf, recv_sem, box_z, buf_z, send_sem, recv_z):
@@ -282,17 +305,13 @@
     total = lax.fori_loop(
         0, 16, lambda i, t: t + buf[i].astype(F32), jnp.zeros((48, 384), F32)
     )
-    box_z[...] = jnp.zeros_like(box_z)
     for z in range(16):
-        box_z[z, 0:3, :] = total[3 * z : 3 * z + 3, :]
+        for r in range(3):
+            box_z[z, :, r * 384 : r * 384 + 384] = total[3 * z + r : 3 * z + r + 1, :]
     buf_z[me.z] = box_z[me.z]
-
-    def step(i, carry):
-        to = lax.rem(me.z + i, 16)
+    for i in (8, 9, 7, 10, 6, 11, 5, 12, 4, 13, 3, 14, 2, 15, 1):
+        to = wrap(me.z + i, 16)
         send(box_z.at[to], buf_z.at[me.z], send_sem, recv_z, me.dp, to * 4 + me.role)
-        return carry
-
-    lax.fori_loop(1, 16, step, 0)
 
 
 def third_weight_sum(me, buf_z, recv_z, rows, send_sem, recv_sem):
@@ -308,9 +327,9 @@
     drain(rows.at[0], recv_sem)
     left, right = rows[0], rows[1]
     first = me.core == 0
-    out[0:1, 0:384] = jnp.where(first, left[0:1], right[1:2])
-    out[0:1, 384:768] = jnp.where(first, right[0:1], left[2:3])
-    out[0:1, 768:1152] = jnp.where(first, left[1:2], right[2:3])
+    out[0:1, 0:384] = jnp.where(first, left[:, 0:384], right[:, 384:768])
+    out[0:1, 384:768] = jnp.where(first, right[:, 0:384], left[:, 768:1152])
+    out[0:1, 768:1152] = jnp.where(first, left[:, 384:768], right[:, 768:1152])
 
 
 def start_back_pair(me, grads, buf, send_sem, recv_sem):
@@ -319,13 +338,12 @@
     buf[me.core] = grads[me.core]
 
 
-def start_back(me, buf, recv_pair, box, out, local_sem, send_sem, recv_sem):
+def fill_back(buf, recv_pair, box):
     drain(buf.at[0], recv_pair)
     r = iota((256, 1), 0)
     at = ((r // 4) % 2) * 128 + (r % 4) * 32 + r // 8
     rows = dot(one_hot(iota((256, 256), 1) == at), buf[...].reshape(256, D))
     box[...] = rows.reshape(32, 8, D).astype(BF16)
-    start_tokens(me, box, out, local_sem, send_sem, recv_sem)
 
 
 def normalize(x):
@@ -516,18 +534,19 @@
     for copy in loads[2:]:
         copy.wait()
     window_units(windows, units)
-    for chunk in range(2):
-        spread_first(me, zbuf, full, chunk, recv_z, w_send.at[1], recv_first)
     pair_sems = (wp_sem.at[0], wp_sem.at[1])
-    for chunk in range(2):
-        spread_second(me, full, chunk, recv_first, w_send.at[2], recv_second, *pair_sems)
-    for chunk in range(2):
-        spread_third(me, full, chunk, recv_second, w_send.at[3], recv_third, *pair_sems)
+    second = (recv_second, *pair_sems)
+    third = (w_send.at[3], recv_third, *pair_sems)
+    spread_first(me, zbuf, full, 0, recv_z, w_send.at[1], recv_first)
+    spread_second(me, full, 0, recv_first, w_send.at[2], *second)
+    spread_first(me, zbuf, full, 1, recv_z, w_send.at[1], recv_first)
+    spread_third(me, full, 0, recv_second, *third)
+    spread_second(me, full, 1, recv_first, w_send.at[4], *second, to=(2, 1, 3))
+    start_tokens(me, upstream, ubuf, local.at[1], tok_send.at[1], tok_recv.at[1], 16, 8)
     wait_tokens(me, video, vbuf, local.at[0], tok_recv.at[0])
     start_pair(me, vbuf, tokens, vbox, pair_send.at[0], pair_recv.at[0])
-    start_tokens(me, upstream, ubuf, local.at[1], tok_send.at[1], tok_recv.at[1])
-    for chunk in range(2):
-        spread_last(me, full, chunk, recv_third, *pair_sems)
+    spread_last(me, full, 0, recv_third, *pair_sems)
+    spread_direct(me, full, 1, recv_second, *pair_sems)
     drain(tokens.at[0], pair_recv.at[0])
     norm_tokens(tokens, scale, bias, order, normed)
     drain(full.at[:, :, 0], wp_sem.at[1])
@@ -536,14 +555,15 @@
     pool_clips(tokens, context, order, full, part)
     start_pooled(me, part, box1, in1, pool_send.at[0], pool_recv.at[0])
     pooled_along_z(me, in1, pool_recv.at[0], buf2, pool_send.at[1], pool_recv.at[1])
+    start_tokens(me, upstream, ubuf, local.at[1], tok_send.at[1], tok_recv.at[1], 7, 1)
+    pooled_in_plane(me, buf2, pool_recv.at[1], pool, pool_send.at[2], pool_recv.at[2])
     wait_tokens(me, upstream, ubuf, local.at[1], tok_recv.at[1])
     start_pair(me, ubuf, ups, ubox, pair_send.at[1], pair_recv.at[1])
-    pooled_in_plane(me, buf2, pool_recv.at[1], pool, pool_send.at[2], pool_recv.at[2])
-    drain(ups.at[0], pair_recv.at[1])
     finish_pooled(pool, pool_recv.at[2], pooled)
     contrast(pooled, units, positives, loss_out, grad_pooled)
     save = pltpu.make_async_copy(pooled, pooled_out, store)
     save.start()
+    drain(ups.at[0], pair_recv.at[1])
     grad_clip = grad_pooled[pl.ds(pl.multiple_of(me.dp * 8, 8), 8), :] * 64.0
     grad_output[...] = spread(ups, grad_clip)
     grad_half = grad_output[...].astype(BF16)
@@ -557,18 +577,20 @@
     backward_attention((2, 3, 4, 5), qkv, prob, grad_context, grad_qkv)
     backward_tokens(tokens, grad_output[...], grad_qkv, full, order, scale, grads)
     start_back_pair(me, grads, pair_buf, out_send.at[0], out_recv.at[0])
-    start_back(
-        me, pair_buf, out_recv.at[0], out_box, video_out, local.at[2], out_send.at[1], out_recv.at[1]
-    )
+    fill_back(pair_buf, out_recv.at[0], out_box)
+    out_sems = (local.at[2], out_send.at[1], out_recv.at[1])
+    start_tokens(me, out_box, video_out, *out_sems, 16, 12)
     second_weight_sum(me, gw_buf, gw_recv.at[1], box_z, buf_z, gw_send.at[2], gw_recv.at[2])
+    start_tokens(me, out_box, video_out, *out_sems, 11, 1)
     third_weight_sum(me, buf_z, gw_recv.at[2], rows, gw_send.at[3], gw_recv.at[3])
     finish_weight_sum(me, rows, gw_recv.at[3], weight_out)
     wait_tokens(me, out_box, video_out, local.at[2], out_recv.at[1])
     save.wait()
     drain(zbuf.at[pl.ds(0, 15)], w_send.at[0])
     drain(full.at[0, pl.ds(0, 3), 0, 0], w_send.at[1])
-    drain(full.at[0, pl.ds(0, 2)], w_send.at[2])
-    drain(full.at[0, 0], w_send.at[3])
+    drain(full.at[0, pl.ds(0, 2), 0], w_send.at[2])
+    drain(full.at[0, 0, 0], w_send.at[3])
+    drain(full.at[0, pl.ds(0, 3), 0], w_send.at[4])
     drain(full.at[:, :, 0], wp_sem.at[0])
     for i in range(2):
         drain(vbuf.at[pl.ds(0, 31)], tok_send.at[i])
@@ -607,10 +629,10 @@
         single(64, D), single(64, D), single(64, D), single(256, D),
         half(256, D), half(256, 3 * D), half(2, 4, 32, D),
         half(2, 16, 48, 384), half(16, 48, 384), half(16, 48, 384), half(16, 48, 384),
-        single(16, 4, 384), single(16, 4, 384), single(2, 4, 384),
+        single(16, 1, 1152), single(16, 1, 1152), single(2, 1, 1152),
         half(2, 4, 32, D), half(32, 8, D),
         dma((6,)), dma((3,)), dma((2,)), dma((2,)), dma((2,)), dma((2,)),
-        dma((4,)), dma((2,)), dma((2, 2)), dma((2, 2, 2)), dma((2, 2, 2)), dma((2,)),
+        dma((5,)), dma((2,)), dma((2, 2)), dma((2, 2, 3)), dma((2, 2, 2)), dma((2,)),
         dma((3,)), dma((3,)), dma((4,)), dma((4,)), dma((2,)), dma((2,)), dma,
     ]
 

time: 122 us -> 114 us (0.934)
  Pallas kernels: 116 us -> 108 us
    pallas_call x1, Pallas kernels: 116 us -> 108 us  [per_device(): pl.pallas_call(kernel, out_shape=[shape(32, 8, D), shape(1, 1152, dtype=F...]
where the time goes in v3:
time: 114 us; the launch traced here: 113 us
  Pallas kernels  108 us (95%)
  local copies, waits for them, and re-layouts  3.08 us (3%)
  between operations  2.41 us (2%)
    pallas_call x1, Pallas kernels, per_device(): pl.pallas_call(kernel, out_shape=[shape(32, 8, D), shape(1, 1152, dtype=F...  108 us
    unnamed x7, local copies, waits for them, and re-layouts  3.08 us

profile of v3, /device:TPU:1, one launch (start us, length us, event | category | flops | bytes accessed | tf_op | source)
XLA Modules:
  0.0 113.4 jit_solution(10502638836438145729)
XLA Ops:
  0.6 107.9 %shard_map.111 = (bf16[32,8,768]{2,1,0:T(8,128)(2,1)}, f32[1,1152]{1,0:T(1,128)}, f32[64,768]{1,0:T(8,128)}, f32[1,1]{1,0:T(1,128)}) custom-call(bf16[32,8,768]{2,1,0:T(8,128)(2,1)} %bitcast.5, bf16[32,8,768]{2,1,0:T(8,128)(2,1)} %bitcast.6, bf16[12,2304]{1,0:T(8,128)(2,1)} %w_qkv.1, bf16[12,768]{1,0:T(8,128)(2,1)} %w_out.1, f32[768]{0:T(1024)} %scale_in.1, ...), custom_call_target="tpu_custom_call" | custom-call | tf_op jit(solution)/shard_map/pallas_call | solution.py:642
  108.6 0.0 copy-start.1
  108.6 0.0 copy-start
  108.6 1.8 %copy.16 = bf16[1,1,256,768]{3,2,1,0:T(8,128)(2,1)} copy(bf16[1,1,256,768]{3,2,1,0:T(8,128)(2,1)} %bitcast.4) | data formatting | bytes 786432
  110.4 0.0 copy-done.1
  110.4 0.6 copy.17
  111.0 0.0 copy-done
  111.0 0.7 copy.18
Async XLA Ops:
  108.6 1.8 %copy-start.1 = (f32[1,1152]{1,0:T(1,128)S(1)}, f32[1,1152]{1,0:T(1,128)}, u32[]{:S(2)}) copy-start(f32[1,1152]{1,0:T(1,128)} %get-tuple-element.17) | copy-start | bytes 13828
  108.6 2.4 %copy-start = (f32[64,768]{1,0:T(8,128)S(1)}, f32[64,768]{1,0:T(8,128)}, u32[]{:S(2)}) copy-start(f32[64,768]{1,0:T(8,128)} %get-tuple-element.18) | copy-start | bytes 589828

commit v4 on v3

--- a/solution.py
+++ b/solution.py
@@ -300,14 +300,18 @@
     send(own.at[me.dp * 2 + other], buf.at[n], send_sem, recv_sem, me.dp, to)
 
 
-def second_weight_sum(me, buf, recv_sem, box_z, buf_z, send_sem, recv_z):
+def second_weight_sum(me, buf, recv_sem, wide, box_z, buf_z, send_sem, recv_z):
     drain(buf.at[pl.ds(0, 15)], recv_sem)
     total = lax.fori_loop(
         0, 16, lambda i, t: t + buf[i].astype(F32), jnp.zeros((48, 384), F32)
     )
+    wide[...] = jnp.zeros_like(wide)
     for z in range(16):
         for r in range(3):
-            box_z[z, :, r * 384 : r * 384 + 384] = total[3 * z + r : 3 * z + r + 1, :]
+            row = total[3 * z + r : 3 * z + r + 1, :]
+            for n in range(3):
+                wide[z, r * 3 + n : r * 3 + n + 1, :] = row[:, n * 128 : n * 128 + 128]
+    box_z[...] = wide[...].astype(BF16)
     buf_z[me.z] = box_z[me.z]
     for i in (8, 9, 7, 10, 6, 11, 5, 12, 4, 13, 3, 14, 2, 15, 1):
         to = wrap(me.z + i, 16)
@@ -316,7 +320,7 @@
 
 def third_weight_sum(me, buf_z, recv_z, rows, send_sem, recv_sem):
     drain(buf_z.at[pl.ds(0, 15)], recv_z)
-    rows[me.core] = jnp.sum(buf_z[...], 0)
+    rows[me.core] = jnp.sum(buf_z[...].astype(F32), 0)
     send(
         rows.at[me.core], rows.at[me.core], send_sem, recv_sem,
         me.dp, me.seq + 1 - 2 * me.core,
@@ -325,11 +329,18 @@
 
 def finish_weight_sum(me, rows, recv_sem, out):
     drain(rows.at[0], recv_sem)
-    left, right = rows[0], rows[1]
+    halves = (rows[0], rows[1])
     first = me.core == 0
-    out[0:1, 0:384] = jnp.where(first, left[:, 0:384], right[:, 384:768])
-    out[0:1, 384:768] = jnp.where(first, right[:, 0:384], left[:, 768:1152])
-    out[0:1, 768:1152] = jnp.where(first, left[:, 384:768], right[:, 768:1152])
+
+    def part(source, row, n):
+        at = row * 3 + n
+        return halves[source][at : at + 1]
+
+    for n in range(3):
+        at = n * 128
+        out[0:1, at : at + 128] = jnp.where(first, part(0, 0, n), part(1, 1, n))
+        out[0:1, 384 + at : 512 + at] = jnp.where(first, part(1, 0, n), part(0, 2, n))
+        out[0:1, 768 + at : 896 + at] = jnp.where(first, part(0, 1, n), part(1, 2, n))
 
 
 def start_back_pair(me, grads, buf, send_sem, recv_sem):
@@ -407,8 +418,10 @@
     return (iota((256, 128), 0) // 32) % 2 == (iota((256, 128), 1) // 32) % 2
 
 
-def norm_tokens(tokens, scale, bias, order, normed):
-    unit, _ = normalize(tokens[...].reshape(256, D).astype(F32))
+def norm_tokens(tokens, scale, bias, order, units, inverses, normed):
+    unit, inverse = normalize(tokens[...].reshape(256, D).astype(F32))
+    units[...] = unit
+    inverses[...] = inverse
     rows = (unit * scale[...].reshape(1, D) + bias[...].reshape(1, D)).astype(BF16)
     normed[...] = dot(rows, order[...]).astype(BF16)
 
@@ -486,14 +499,14 @@
             put_rows(grad_qkv, u, columns[2], grad_value)
 
 
-def backward_tokens(tokens, grad_output, grad_qkv, full, order, scale, out):
+def backward_tokens(units, inverses, grad_output, grad_qkv, full, order, scale, out):
     back = jnp.zeros((256, D), F32)
     for n in range(6):
         weight = full[n // 4, n % 4].reshape(D, 384)
         back = back + dot_nt(grad_qkv[:, n * 384 : n * 384 + 384], weight)
     grad_normed = dot_nt(back.astype(BF16), order[...])
     scaled = grad_normed * scale[...].reshape(1, D)
-    unit, inverse = normalize(tokens[...].reshape(256, D).astype(F32))
+    unit, inverse = units[...], inverses[...]
     grad_norm = inverse * (
         scaled
         - jnp.mean(scaled, -1, keepdims=True)
@@ -508,7 +521,8 @@
     wq, wo, scale, bias, windows, positives, order, scatter,
     vbuf, ubuf, vbox, ubox, tokens, ups, zbuf, full, normed, qkv, prob, context, part,
     box1, in1, buf2, pool, pooled, units, grad_pooled, grad_output, grad_context, grad_qkv, grads,
-    box, gw_pair, gw_own, gw_buf, box_z, buf_z, rows, pair_buf, out_box,
+    box, gw_pair, gw_own, gw_buf, wide, box_z, buf_z, rows, pair_buf, out_box,
+    token_unit, token_inverse,
     load, local, tok_send, tok_recv, pair_send, pair_recv,
     w_send, recv_z, recv_first, recv_second, recv_third, wp_sem,
     pool_send, pool_recv, gw_send, gw_recv, out_send, out_recv, store,
@@ -548,7 +562,7 @@
     spread_last(me, full, 0, recv_third, *pair_sems)
     spread_direct(me, full, 1, recv_second, *pair_sems)
     drain(tokens.at[0], pair_recv.at[0])
-    norm_tokens(tokens, scale, bias, order, normed)
+    norm_tokens(tokens, scale, bias, order, token_unit, token_inverse, normed)
     drain(full.at[:, :, 0], wp_sem.at[1])
     project(normed, full, qkv)
     attend(qkv, prob, context)
@@ -575,12 +589,12 @@
         me, box, gw_pair, gw_recv.at[0], gw_own, gw_buf, gw_send.at[1], gw_recv.at[1]
     )
     backward_attention((2, 3, 4, 5), qkv, prob, grad_context, grad_qkv)
-    backward_tokens(tokens, grad_output[...], grad_qkv, full, order, scale, grads)
+    backward_tokens(token_unit, token_inverse, grad_output[...], grad_qkv, full, order, scale, grads)
     start_back_pair(me, grads, pair_buf, out_send.at[0], out_recv.at[0])
     fill_back(pair_buf, out_recv.at[0], out_box)
     out_sems = (local.at[2], out_send.at[1], out_recv.at[1])
     start_tokens(me, out_box, video_out, *out_sems, 16, 12)
-    second_weight_sum(me, gw_buf, gw_recv.at[1], box_z, buf_z, gw_send.at[2], gw_recv.at[2])
+    second_weight_sum(me, gw_buf, gw_recv.at[1], wide, box_z, buf_z, gw_send.at[2], gw_recv.at[2])
     start_tokens(me, out_box, video_out, *out_sems, 11, 1)
     third_weight_sum(me, buf_z, gw_recv.at[2], rows, gw_send.at[3], gw_recv.at[3])
     finish_weight_sum(me, rows, gw_recv.at[3], weight_out)
@@ -610,6 +624,20 @@
     return jax.ShapeDtypeStruct(dims, dtype)
 
 
+def keep(*refs):
+    n = 4
+    ins, outs, held, sems = refs[:n], refs[n : 2 * n], refs[2 * n : 3 * n], refs[3 * n]
+    reads = [pltpu.make_async_copy(ins[i], held[i], sems.at[0, i]) for i in range(n)]
+    writes = [pltpu.make_async_copy(held[i], outs[i], sems.at[1, i]) for i in range(n)]
+    for copy in reads:
+        copy.start()
+    for read, write in zip(reads, writes):
+        read.wait()
+        write.start()
+    for copy in writes:
+        copy.wait()
+
+
 def scratch_shapes():
     dma = pltpu.SemaphoreType.DMA
 
@@ -629,8 +657,8 @@
         single(64, D), single(64, D), single(64, D), single(256, D),
         half(256, D), half(256, 3 * D), half(2, 4, 32, D),
         half(2, 16, 48, 384), half(16, 48, 384), half(16, 48, 384), half(16, 48, 384),
-        single(16, 1, 1152), single(16, 1, 1152), single(2, 1, 1152),
-        half(2, 4, 32, D), half(32, 8, D),
+        single(16, 16, 128), half(16, 16, 128), half(16, 16, 128), single(2, 16, 128),
+        half(2, 4, 32, D), half(32, 8, D), single(256, D), single(256, 1),
         dma((6,)), dma((3,)), dma((2,)), dma((2,)), dma((2,)), dma((2,)),
         dma((5,)), dma((2,)), dma((2, 2)), dma((2, 2, 3)), dma((2, 2, 2)), dma((2,)),
         dma((3,)), dma((3,)), dma((4,)), dma((4,)), dma((2,)), dma((2,)), dma,
@@ -655,6 +683,15 @@
         video.reshape(32, 8, D), upstream.reshape(32, 8, D), w_qkv, w_out,
         standardize_scale, ln_bias, windows, positives,
     )
+    results = (grad_video, grad_out_weight, pooled, loss)
+    grad_video, grad_out_weight, pooled, loss = pl.pallas_call(
+        keep,
+        out_shape=[jax.ShapeDtypeStruct(a.shape, a.dtype) for a in results],
+        in_specs=[anywhere] * 4,
+        out_specs=[anywhere] * 4,
+        scratch_shapes=[pltpu.VMEM(a.shape, a.dtype) for a in results]
+        + [pltpu.SemaphoreType.DMA((2, 4))],
+    )(*results)
     return grad_video.reshape(1, 1, 256, D), grad_out_weight, pooled, loss.reshape(())
 
 

time: 114 us -> 111 us (0.974)
  local copies, waits for them, and re-layouts: 3.08 us -> 0 us
  Pallas kernels: 108 us -> 110 us
  between operations: 2.41 us -> 0.64 us
    unnamed x7 -> x0, local copies, waits for them, and re-layouts: 3.08 us -> none
    pallas_call x0 -> x1, Pallas kernels: none -> 2.44 us  [per_device(): pl.pallas_call(keep, out_shape=[jax.ShapeDtypeStruct(a.shape, a.dtype) fo...]
where the time goes in v4:
time: 111 us
  Pallas kernels  110 us (99%)
    pallas_call x1, Pallas kernels, per_device(): pl.pallas_call(kernel, out_shape=[shape(32, 8, D), shape(1, 1152, dtype=F...  108 us
    pallas_call x1, Pallas kernels, per_device(): pl.pallas_call(keep, out_shape=[jax.ShapeDtypeStruct(a.shape, a.dtype) fo...  2.44 us

profile of v4, /device:TPU:1, one launch (start us, length us, event | category | flops | bytes accessed | tf_op | source)
XLA Modules:
  0.0 110.6 jit_solution(10528528224331980834)
XLA Ops:
  0.6 107.5 %shard_map.111 = (bf16[32,8,768]{2,1,0:T(8,128)(2,1)}, f32[1,1152]{1,0:T(1,128)}, f32[64,768]{1,0:T(8,128)}, f32[1,1]{1,0:T(1,128)}) custom-call(bf16[32,8,768]{2,1,0:T(8,128)(2,1)} %bitcast.4, bf16[32,8,768]{2,1,0:T(8,128)(2,1)} %bitcast.5, bf16[12,2304]{1,0:T(8,128)(2,1)} %w_qkv.1, bf16[12,768]{1,0:T(8,128)(2,1)} %w_out.1, f32[768]{0:T(1024)} %scale_in.1, ...), custom_call_target="tpu_custom_call" | custom-call | tf_op jit(solution)/shard_map/pallas_call | solution.py:670
  108.1 2.4 %shard_map.112 = (bf16[32,8,768]{2,1,0:T(8,128)(2,1)}, f32[1,1152]{1,0:T(1,128)}, f32[64,768]{1,0:T(8,128)}, f32[1,1]{1,0:T(1,128)}) custom-call(bf16[32,8,768]{2,1,0:T(8,128)(2,1)} %get-tuple-element.12.refs_0_, f32[1,1152]{1,0:T(1,128)} %get-tuple-element.13.refs_1_, f32[64,768]{1,0:T(8,128)} %get-tuple-element.14.refs_2_, f32[1,1]{1,0:T(1,128)} %get-tuple-element.15.refs_3_), custom_call_target="tpu_custom_call" | custom-call | tf_op jit(solution)/shard_map/pallas_call | solution.py:687

commit v5 on v4

--- a/solution.py
+++ b/solution.py
@@ -552,11 +552,11 @@
     second = (recv_second, *pair_sems)
     third = (w_send.at[3], recv_third, *pair_sems)
     spread_first(me, zbuf, full, 0, recv_z, w_send.at[1], recv_first)
+    start_tokens(me, upstream, ubuf, local.at[1], tok_send.at[1], tok_recv.at[1], 16, 8)
     spread_second(me, full, 0, recv_first, w_send.at[2], *second)
     spread_first(me, zbuf, full, 1, recv_z, w_send.at[1], recv_first)
     spread_third(me, full, 0, recv_second, *third)
     spread_second(me, full, 1, recv_first, w_send.at[4], *second, to=(2, 1, 3))
-    start_tokens(me, upstream, ubuf, local.at[1], tok_send.at[1], tok_recv.at[1], 16, 8)
     wait_tokens(me, video, vbuf, local.at[0], tok_recv.at[0])
     start_pair(me, vbuf, tokens, vbox, pair_send.at[0], pair_recv.at[0])
     spread_last(me, full, 0, recv_third, *pair_sems)

time: 111 us -> 111 us (level)
  no operation moved by 1% of the time
where the time goes in v5:
time: 111 us
  Pallas kernels  110 us (99%)
    pallas_call x1, Pallas kernels, per_device(): pl.pallas_call(kernel, out_shape=[shape(32, 8, D), shape(1, 1152, dtype=F...  108 us
    pallas_call x1, Pallas kernels, per_device(): pl.pallas_call(keep, out_shape=[jax.ShapeDtypeStruct(a.shape, a.dtype) fo...  2.44 us

profile of v5, /device:TPU:1, one launch (start us, length us, event | category | flops | bytes accessed | tf_op | source)
XLA Modules:
  0.0 110.6 jit_solution(8707916346524332693)
XLA Ops:
  0.6 107.5 %shard_map.111 = (bf16[32,8,768]{2,1,0:T(8,128)(2,1)}, f32[1,1152]{1,0:T(1,128)}, f32[64,768]{1,0:T(8,128)}, f32[1,1]{1,0:T(1,128)}) custom-call(bf16[32,8,768]{2,1,0:T(8,128)(2,1)} %bitcast.4, bf16[32,8,768]{2,1,0:T(8,128)(2,1)} %bitcast.5, bf16[12,2304]{1,0:T(8,128)(2,1)} %w_qkv.1, bf16[12,768]{1,0:T(8,128)(2,1)} %w_out.1, f32[768]{0:T(1024)} %scale_in.1, ...), custom_call_target="tpu_custom_call" | custom-call | tf_op jit(solution)/shard_map/pallas_call | solution.py:670
  108.2 2.4 %shard_map.112 = (bf16[32,8,768]{2,1,0:T(8,128)(2,1)}, f32[1,1152]{1,0:T(1,128)}, f32[64,768]{1,0:T(8,128)}, f32[1,1]{1,0:T(1,128)}) custom-call(bf16[32,8,768]{2,1,0:T(8,128)(2,1)} %get-tuple-element.12.refs_0_, f32[1,1152]{1,0:T(1,128)} %get-tuple-element.13.refs_1_, f32[64,768]{1,0:T(8,128)} %get-tuple-element.14.refs_2_, f32[1,1]{1,0:T(1,128)} %get-tuple-element.15.refs_3_), custom_call_target="tpu_custom_call" | custom-call | tf_op jit(solution)/shard_map/pallas_call | solution.py:687

commit v6 on v5

--- a/solution.py
+++ b/solution.py
@@ -166,12 +166,14 @@
     return (x // 2) * 4 + me.y, me.z * 4 + (x % 2) * 2 + me.core
 
 
-def spread_first(me, zbuf, full, chunk, recv_z, send_sem, recv):
+def spread_first(me, zbuf, wide_rows, full, chunk, recv_z, send_sem, recv):
     drain(zbuf.at[pl.ds(0, 7 + chunk)], recv_z.at[chunk])
     r = iota((96, 1), 0)
     pick = one_hot(iota((96, 128), 1) == (r // 12) * 16 + r % 12)
-    rows = zbuf[chunk * 8 : chunk * 8 + 8].reshape(128, 384)
-    block = dot(pick, rows).astype(BF16)
+    wide_rows[...] = jnp.zeros_like(wide_rows)
+    for j in range(8):
+        wide_rows[j, 0:12, :] = zbuf[chunk * 8 + j].astype(F32)
+    block = dot(pick, wide_rows[...].reshape(128, 384).astype(BF16)).astype(BF16)
     full[me.x_hi, me.y, me.core, chunk, me.x_lo] = block.reshape(2, 48, 384)
     a = full.at[me.x_hi, me.y, me.core, chunk, me.x_lo, 0]
     b = full.at[me.x_hi, me.y, me.core, chunk, me.x_lo, 1]
@@ -522,7 +524,7 @@
     vbuf, ubuf, vbox, ubox, tokens, ups, zbuf, full, normed, qkv, prob, context, part,
     box1, in1, buf2, pool, pooled, units, grad_pooled, grad_output, grad_context, grad_qkv, grads,
     box, gw_pair, gw_own, gw_buf, wide, box_z, buf_z, rows, pair_buf, out_box,
-    token_unit, token_inverse,
+    token_unit, token_inverse, wide_rows,
     load, local, tok_send, tok_recv, pair_send, pair_recv,
     w_send, recv_z, recv_first, recv_second, recv_third, wp_sem,
     pool_send, pool_recv, gw_send, gw_recv, out_send, out_recv, store,
@@ -539,7 +541,7 @@
     column = pl.multiple_of(lax.rem(me.dp, 6) * 384, 384)
     column_out = pl.multiple_of(lax.rem(me.dp, 2) * 384, 384)
     piece = jnp.where(me.dp < 6, wq[:, pl.ds(column, 384)], wo[:, pl.ds(column_out, 384)])
-    zbuf[0] = jnp.concatenate([piece.astype(F32), jnp.zeros((4, 384), F32)], 0).astype(BF16)
+    zbuf[0] = piece
     arrive()
     start_weights(me, zbuf, w_send.at[0], recv_z)
     start_tokens(me, video, vbuf, local.at[0], tok_send.at[0], tok_recv.at[0])
@@ -551,10 +553,10 @@
     pair_sems = (wp_sem.at[0], wp_sem.at[1])
     second = (recv_second, *pair_sems)
     third = (w_send.at[3], recv_third, *pair_sems)
-    spread_first(me, zbuf, full, 0, recv_z, w_send.at[1], recv_first)
+    spread_first(me, zbuf, wide_rows, full, 0, recv_z, w_send.at[1], recv_first)
     start_tokens(me, upstream, ubuf, local.at[1], tok_send.at[1], tok_recv.at[1], 16, 8)
     spread_second(me, full, 0, recv_first, w_send.at[2], *second)
-    spread_first(me, zbuf, full, 1, recv_z, w_send.at[1], recv_first)
+    spread_first(me, zbuf, wide_rows, full, 1, recv_z, w_send.at[1], recv_first)
     spread_third(me, full, 0, recv_second, *third)
     spread_second(me, full, 1, recv_first, w_send.at[4], *second, to=(2, 1, 3))
     wait_tokens(me, video, vbuf, local.at[0], tok_recv.at[0])
@@ -651,14 +653,14 @@
         half(12, 3 * D), half(12, D), single(D), single(D), single(64, D),
         pltpu.VMEM((64,), jnp.int32), half(D, D), half(D, D),
         half(32, 8, D), half(32, 8, D), half(4, 32, D), half(4, 32, D),
-        half(2, 4, 32, D), half(2, 4, 32, D), half(16, 16, 384), half(2, 4, 2, 2, 2, 2, 48, 384),
+        half(2, 4, 32, D), half(2, 4, 32, D), half(16, 12, 384), half(2, 4, 2, 2, 2, 2, 48, 384),
         half(256, D), half(256, 3 * D), single(12, 256, 128), half(256, D), single(8, D),
         single(4, 2, D), single(4, 2, D), single(16, 2, D), single(32, 2, D),
         single(64, D), single(64, D), single(64, D), single(256, D),
         half(256, D), half(256, 3 * D), half(2, 4, 32, D),
         half(2, 16, 48, 384), half(16, 48, 384), half(16, 48, 384), half(16, 48, 384),
         single(16, 16, 128), half(16, 16, 128), half(16, 16, 128), single(2, 16, 128),
-        half(2, 4, 32, D), half(32, 8, D), single(256, D), single(256, 1),
+        half(2, 4, 32, D), half(32, 8, D), single(256, D), single(256, 1), single(8, 16, 384),
         dma((6,)), dma((3,)), dma((2,)), dma((2,)), dma((2,)), dma((2,)),
         dma((5,)), dma((2,)), dma((2, 2)), dma((2, 2, 3)), dma((2, 2, 2)), dma((2,)),
         dma((3,)), dma((3,)), dma((4,)), dma((4,)), dma((2,)), dma((2,)), dma,

time: 111 us -> 111 us (level)
  no operation moved by 1% of the time
where the time goes in v6:
time: 111 us
  Pallas kernels  110 us (99%)
    pallas_call x1, Pallas kernels, per_device(): pl.pallas_call(kernel, out_shape=[shape(32, 8, D), shape(1, 1152, dtype=F...  108 us
    pallas_call x1, Pallas kernels, per_device(): pl.pallas_call(keep, out_shape=[jax.ShapeDtypeStruct(a.shape, a.dtype) fo...  2.44 us

profile of v6, /device:TPU:1, one launch (start us, length us, event | category | flops | bytes accessed | tf_op | source)
XLA Modules:
  0.0 110.6 jit_solution(11814626516762270790)
XLA Ops:
  0.6 107.5 %shard_map.111 = (bf16[32,8,768]{2,1,0:T(8,128)(2,1)}, f32[1,1152]{1,0:T(1,128)}, f32[64,768]{1,0:T(8,128)}, f32[1,1]{1,0:T(1,128)}) custom-call(bf16[32,8,768]{2,1,0:T(8,128)(2,1)} %bitcast.4, bf16[32,8,768]{2,1,0:T(8,128)(2,1)} %bitcast.5, bf16[12,2304]{1,0:T(8,128)(2,1)} %w_qkv.1, bf16[12,768]{1,0:T(8,128)(2,1)} %w_out.1, f32[768]{0:T(1024)} %scale_in.1, ...), custom_call_target="tpu_custom_call" | custom-call | tf_op jit(solution)/shard_map/pallas_call | solution.py:672
  108.2 2.4 %shard_map.112 = (bf16[32,8,768]{2,1,0:T(8,128)(2,1)}, f32[1,1152]{1,0:T(1,128)}, f32[64,768]{1,0:T(8,128)}, f32[1,1]{1,0:T(1,128)}) custom-call(bf16[32,8,768]{2,1,0:T(8,128)(2,1)} %get-tuple-element.12.refs_0_, f32[1,1152]{1,0:T(1,128)} %get-tuple-element.13.refs_1_, f32[64,768]{1,0:T(8,128)} %get-tuple-element.14.refs_2_, f32[1,1]{1,0:T(1,128)} %get-tuple-element.15.refs_3_), custom_call_target="tpu_custom_call" | custom-call | tf_op jit(solution)/shard_map/pallas_call | solution.py:689
